TPU v7x, 32 devices: a whole 2x2x4 slice. The times are simulated.
32 devices in a mesh: groups: 2 (over y), seq: 4 (over z), slide: 2 (over x), head: 2 (over core).
Axes of the slice: x: 2, y: 2, z: 4, core: 2. Of those that a mesh axis runs over, the one named last changes fastest.
Arguments:
- latents: bfloat16 [1024, 1024], P(('groups', 'seq'), 'head'), parts along dimension 0, may hold values from -153 to 153
- tile_keys: bfloat16 [4, 1024, 1024], P(('groups', 'slide'), 'seq', 'head'), parts along dimension 0, may hold values from -6 to 6
- tile_values: bfloat16 [4, 1024, 1024], P(('groups', 'slide'), 'seq', 'head'), parts along dimension 0, may hold values from -24 to 24
- tile_mask: int32 [4, 8], P(('groups', 'slide'), 'seq'), parts along dimension 0, may hold values from 0 to 1, as said below
- latent_counts: int32 [4], P(('groups', 'slide')), parts along dimension 0, may hold values from 128 to 512
- out_weight: bfloat16 [1024, 1024], P('head'), may hold values from -0.1875 to 0.1875
- cotangent: bfloat16 [4, 512, 1024], P(('groups', 'slide'), 'seq'), parts along dimension 0, may hold values from -6 to 6
Outputs:
- pooled: bfloat16 [4, 512, 1024], P(('groups', 'slide'), 'seq', 'head'), parts along dimension 0
- grad_latents: float32 [1024, 1024], P(('groups', 'seq'), 'head'), parts along dimension 0
- grad_keys: bfloat16 [4, 1024, 1024], P(('groups', 'slide'), 'seq', 'head'), parts along dimension 0
- grad_values: bfloat16 [4, 1024, 1024], P(('groups', 'slide'), 'seq', 'head'), parts along dimension 0
There are 2 independent parts, one for each index of `groups`. A program takes and returns all parts, laid end to end along the dimension named above; an argument that names none is the same for every part. Nothing has to cross between parts.
Inputs may be any that keep to these rules, and one draw needn't show every extreme that they name: `tile_mask`: every slide has at least one block of 128 tiles marked 1.
All inputs are finite; a program needn't handle non-finite values.
Results may differ from a plain program's by a relative error of at most 0.035.
Values may be sent and summed in bfloat16 or wider, within the bound.
A program may use at most 64 MiB of HBM per device.

v0:
```python
import jax
import jax.numpy as jnp
from jax import lax
from jax.sharding import PartitionSpec as P

HD = 64
BLOCK = 128


masked_score = -1e30


def body(latents, tile_keys, tile_values, tile_mask, latent_counts, out_weight, cotangent):
    local_rows = latents.shape[0]
    local_width = latents.shape[1]
    head_count = local_width // HD
    factor = HD ** (-0.5)
    queries = lax.all_gather(latents, "seq", axis=0, tiled=True)
    total_rows = queries.shape[0]
    first_row = lax.axis_index("seq") * local_rows
    every_row = lax.broadcasted_iota(jnp.int32, (total_rows, 1), 0)
    own_row = lax.broadcasted_iota(jnp.int32, (local_rows, 1), 0) + first_row
    tile_count = tile_keys.shape[1]
    key_block = tile_keys[0]
    value_block = tile_values[0]
    valid_tiles = jnp.broadcast_to(tile_mask[0][:, None] > 0, (tile_count // BLOCK, BLOCK)).reshape(
        1, tile_count
    )
    live_count = latent_counts[0]
    score_list = []
    for which_head in range(head_count):
        columns = slice(which_head * HD, (which_head + 1) * HD)
        raw_scores = (
            jnp.einsum(
                "qc,tc->qt",
                queries[:, columns],
                key_block[:, columns],
                preferred_element_type=jnp.float32,
            )
            * factor
        )
        score_list.append(jnp.where(valid_tiles, raw_scores, masked_score))
    local_top = jnp.stack([jnp.max(scored, axis=1) for scored in score_list], axis=1)
    row_top = lax.pmax(local_top, "seq")
    expo_list = []
    weighted_list = []
    total_list = []
    for which_head in range(head_count):
        columns = slice(which_head * HD, (which_head + 1) * HD)
        expos = jnp.where(
            valid_tiles,
            jnp.exp(score_list[which_head] - row_top[:, which_head : which_head + 1]),
            0.0,
        )
        expo_list.append(expos)
        total_list.append(jnp.sum(expos, axis=1))
        weighted_list.append(
            jnp.dot(
                expos.astype(jnp.bfloat16),
                value_block[:, columns],
                preferred_element_type=jnp.float32,
            )
        )
    partial_sums = jnp.concatenate(weighted_list, axis=1)
    partial_totals = jnp.stack(total_list, axis=1)
    weighted, totals = lax.psum((partial_sums, partial_totals), "seq")
    span = weighted.shape[0]
    attended = jnp.where(
        every_row < live_count,
        (weighted.reshape(span, head_count, HD) / totals[:, :, None]).reshape(span, local_width),
        0.0,
    ).astype(jnp.bfloat16)
    own_attended = lax.dynamic_slice_in_dim(attended, first_row, local_rows, 0)
    pooled_part = jnp.dot(own_attended, out_weight, preferred_element_type=jnp.float32)
    pooled_parts = [
        lax.psum_scatter(pooled_part.astype(jnp.bfloat16), "head", scatter_dimension=1, tiled=True)
    ]
    projected = jnp.einsum(
        "rd,cd->rc", cotangent[0], out_weight, preferred_element_type=jnp.float32
    )
    upstream = jnp.where(own_row < live_count, projected, 0.0).astype(jnp.bfloat16)
    upstream_all = lax.all_gather(upstream, "seq", axis=0, tiled=True)
    row_delta = jnp.sum(
        (upstream_all.astype(jnp.float32) * attended.astype(jnp.float32)).reshape(
            total_rows, head_count, HD
        ),
        axis=2,
    )
    query_list = []
    key_list = []
    value_list = []
    for which_head in range(head_count):
        columns = slice(which_head * HD, (which_head + 1) * HD)
        up_head = upstream_all[:, columns]
        weights = expo_list[which_head] / totals[:, which_head : which_head + 1]
        value_list.append(
            jnp.einsum(
                "qt,qc->tc",
                weights.astype(jnp.bfloat16),
                up_head,
                preferred_element_type=jnp.float32,
            )
        )
        grad_prob = jnp.einsum(
            "qc,tc->qt", up_head, value_block[:, columns], preferred_element_type=jnp.float32
        )
        grad_score = (
            weights * (grad_prob - row_delta[:, which_head : which_head + 1]) * factor
        ).astype(jnp.bfloat16)
        query_list.append(
            jnp.dot(grad_score, key_block[:, columns], preferred_element_type=jnp.float32)
        )
        key_list.append(
            jnp.einsum(
                "qt,qc->tc", grad_score, queries[:, columns], preferred_element_type=jnp.float32
            )
        )
    grad_rows = jnp.concatenate(query_list, axis=1)
    key_grads = [jnp.concatenate(key_list, axis=1).astype(jnp.bfloat16)]
    value_grads = [jnp.concatenate(value_list, axis=1).astype(jnp.bfloat16)]
    own_grad = lax.psum_scatter(
        grad_rows.astype(jnp.bfloat16), "seq", scatter_dimension=0, tiled=True
    )
    grad_latents = lax.psum(own_grad, "slide").astype(jnp.float32)
    return (
        jnp.stack(pooled_parts, axis=0),
        grad_latents,
        jnp.stack(key_grads, axis=0),
        jnp.stack(value_grads, axis=0),
    )


def solution(mesh):
    placed = (
        P(("groups", "seq"), "head"),
        P(("groups", "slide"), "seq", "head"),
        P(("groups", "slide"), "seq", "head"),
        P(("groups", "slide"), "seq"),
        P(("groups", "slide")),
        P("head", None),
        P(("groups", "slide"), "seq", None),
    )
    return jax.shard_map(
        body,
        mesh=mesh,
        in_specs=placed,
        out_specs=(
            P(("groups", "slide"), "seq", "head"),
            P(("groups", "seq"), "head"),
            P(("groups", "slide"), "seq", "head"),
            P(("groups", "slide"), "seq", "head"),
        ),
        check_vma=False,
    )
```

profile of v0, /device:TPU:0, one launch (start us, length us, event | category | flops | bytes accessed | tf_op | source)
XLA Modules:
  0.0 189.7 jit_solution(3926986250691564147)
XLA Ops:
  7.2 0.7 compare_bitcast_fusion
  8.0 17.7 %all_gather.6 = bf16[512,512]{1,0:T(8,128)(2,1)S(1)} all-gather(bf16[128,512]{1,0:T(8,128)(2,1)} %param.7), channel_id=1, replica_groups=mesh['groups'=2,'seq'=4,'slide'=2,'head'=2] {'seq'}, dimensions={0}, use_global_device_ids=true | all-gather | bytes 655360 | tf_op jit(solution)/shard_map/all_gather | solution.py:18
  25.7 0.3 fusion.233
  26.3 0.3 fusion.231
  26.6 1.0 fusion.230
  27.7 1.1 fusion.229
  28.8 1.1 fusion.228
  29.8 1.1 fusion.227
  30.9 1.1 fusion.226
  32.0 19.5 %pmax.7 = f32[512,8]{0,1:T(8,128)S(1)} all-reduce(f32[512,8]{0,1:T(8,128)S(1)} %stack.67), channel_id=1, replica_groups=mesh['groups'=2,'seq'=4,'slide'=2,'head'=2] {'seq'}, use_global_device_ids=true, to_apply=%region_8.9 | all-reduce | flops 4096 | bytes 32768 | tf_op jit(solution)/shard_map/pmax | solution.py:44
  51.6 2.0 %convolution_dynamic-update-slice_fusion.7 = f32[512,512]{0,1:T(8,128)} fusion(f32[512,256]{0,1:T(8,128)} %get-tuple-element.51, f32[512]{0:T(512)S(1)} %bitcast.205, pred[256]{0:T(512)(128)(4,1)S(1)} %broadcast_bitcast_fusion, bf16[256,512]{1,0:T(8,128)(2,1)S(1)} %bitcast.161), kind=kOutput, calls=%fused_computation.57 | convolution fusion | flops 17170432 | bytes 723456 | tf_op jit(solution)/shard_map/dot_general | solution.py:58
  53.6 0.9 convolution_dynamic-update-slice_fusion.6
  54.6 0.9 convolution_dynamic-update-slice_fusion.5
  55.6 0.9 convolution_dynamic-update-slice_fusion.4
  56.6 0.9 convolution_dynamic-update-slice_fusion.3
  57.5 0.9 convolution_dynamic-update-slice_fusion.2
  58.4 0.9 convolution_dynamic-update-slice_fusion.1
  59.3 0.9 convolution_dynamic-update-slice_fusion
  60.4 2.5 %fusion.97 = (f32[512]{0:T(512)S(1)}, f32[512]{0:T(512)S(1)}, f32[512]{0:T(512)S(1)}, f32[512]{0:T(512)S(1)}, f32[512]{0:T(512)S(1)}, /*index=5*/f32[512]{0:T(512)S(1)}, f32[512]{0:T(512)S(1)}, f32[512]{0:T(512)S(1)}) fusion(f32[512,256]{0,1:T(8,128)S(1)} %get-tuple-element.65, f32[512]{0:T(512)S(1)} %bitcast.182, ...), kind=kLoop, calls=%fused_computation.158 | loop fusion | flops 3141632 | bytes 4227328 | tf_op jit(solution)/shard_map/reduce_sum | solution.py:56
  63.5 1.4 fusion.32
  64.9 20.8 %all_gather.7 = bf16[512,512]{0,1:T(8,128)(2,1)S(1)} all-gather(bf16[128,512]{0,1:T(8,128)(2,1)S(1)} %fusion.32), channel_id=1, replica_groups=mesh['groups'=2,'seq'=4,'slide'=2,'head'=2] {'seq'}, dimensions={0}, use_global_device_ids=true | all-gather | bytes 655360 | tf_op jit(solution)/shard_map/all_gather | solution.py:82
  85.7 19.9 %psum.22 = f32[512,8]{0,1:T(8,128)S(1)} all-reduce(f32[512,8]{0,1:T(8,128)S(1)} %stack.76), channel_id=1, replica_groups=mesh['groups'=2,'seq'=4,'slide'=2,'head'=2] {'seq'}, use_global_device_ids=true, to_apply=%region_18.19 | all-reduce | flops 4096 | bytes 32768 | tf_op jit(solution)/shard_map/psum | solution.py:66
  105.6 2.0 %fusion.42 = bf16[1,256,512]{1,2,0:T(8,128)(2,1)} fusion(bf16[512,512]{0,1:T(8,128)(2,1)S(1)} %all_gather.7, f32[512,256]{0,1:T(8,128)} %get-tuple-element.51, f32[512]{0:T(512)S(1)} %bitcast.231, f32[512]{0:T(512)S(1)} %bitcast.207, pred[256]{0:T(512)(128)(4,1)S(1)} %broadcast_bitcast_fusion), kind=kOutput, calls=%fused_computation.92 | convolution fusion | flops 17317888 | bytes 627200 | tf_op jit(solution)/shard_map/qt,qc->tc/dot_general | solution.py:97
  107.6 0.9 fusion.44
  108.7 0.9 fusion.46
  109.7 0.9 fusion.48
  110.7 0.9 fusion.50
  111.8 0.9 fusion.52
  112.7 0.9 fusion.54
  113.6 0.9 fusion.56
  114.5 1.8 copy.46
  116.3 2.3 %bitcast_reduce_fusion = (f32[512,8]{0,1:T(8,128)S(1)}, bf16[512,512]{0,1:T(8,128)(2,1)}) fusion(bf16[512,512]{0,1:T(8,128)(2,1)S(1)} %all_gather.7, f32[512,512]{0,1:T(8,128)} %all-reduce.3.cloned.1.call-done, f32[512,8]{0,1:T(8,128)S(1)} %psum.22, pred[512]{0:T(512)(128)(4,1)S(1)} %iota_compare_fusion), kind=kLoop, calls=%fused_computation.123 | loop fusion | flops 1830912 | bytes 2130432 | tf_op jit(solution)/shard_map/reduce_sum | solution.py:83
  118.9 0.8 copy-done.15
  119.7 0.3 fusion.30
  120.0 0.7 copy-done.12
  121.0 0.8 copy-done.9
  121.8 0.3 fusion.28
  122.1 0.7 copy-done.6
  123.1 0.8 copy-done.3
  123.8 0.3 fusion.26
  124.1 0.6 copy-done.31
  124.8 0.3 fusion.24
  125.4 0.7 copy-done.29
  126.3 0.3 fusion.39
  126.8 0.3 fusion.37
  127.3 0.3 fusion.35
  127.8 0.3 fusion.33
  128.0 1.0 copy.56
  129.1 0.9 copy-done.21
  130.2 0.3 fusion.60
  130.5 0.7 copy-done.25
  131.4 0.7 copy-done.27
  132.1 0.3 fusion.64
  132.4 0.7 copy-done.33
  133.1 2.0 %convolution_convert_fusion = bf16[128,1024]{1,0:T(8,128)(2,1)} fusion(bf16[512,1024]{1,0:T(8,128)(2,1)S(1)} %copy-done, bf16[512,512]{0,1:T(8,128)(2,1)} %get-tuple-element.25, s32[]{:T(128)S(6)} %select_n.77), kind=kOutput, calls=%fused_computation.48 | convolution fusion | flops 134348800 | bytes 1441796 | tf_op jit(solution)/shard_map/dot_general | solution.py:74
  135.1 14.9 %reduce-scatter.7.cloned.1.call-done = bf16[128,512]{1,0:T(8,128)(2,1)} async-done(((bf16[512,512]{1,0:T(8,128)(2,1)}), bf16[128,512]{1,0:T(8,128)(2,1)}) %reduce-scatter.7.cloned.1.call-update) | async-done | bytes 131088
  150.0 1.7 copy.57
  152.0 0.3 reduce-scatter.5.cloned.1.call-update
  152.3 0.4 copy-done.17
  153.1 0.3 fusion.72
  153.4 0.9 copy.45
  154.3 18.4 %all-reduce.5.cloned.1.call-done = bf16[128,512]{0,1:T(8,128)(2,1)} async-done(((bf16[128,512]{0,1:T(8,128)(2,1)}), bf16[128,512]{0,1:T(8,128)(2,1)}) %all-reduce.5.cloned.1.call-update) | async-done | bytes 131088 | tf_op jit(solution)/shard_map/psum | solution.py:124
  172.7 1.7 copy.44
  174.4 8.7 %reduce-scatter.5.cloned.1.call-done = bf16[128,512]{1,0:T(8,128)(2,1)} async-done(((bf16[128,1024]{1,0:T(8,128)(2,1)}), bf16[128,512]{1,0:T(8,128)(2,1)}) %reduce-scatter.5.cloned.1.call-update) | async-done | bytes 131088 | tf_op jit(solution)/shard_map/reduce_scatter | solution.py:76
  (88 shorter events, 4.5 us)
Async XLA Ops:
  7.2 56.3 %copy-start = (bf16[512,1024]{1,0:T(8,128)(2,1)S(1)}, bf16[512,1024]{1,0:T(8,128)(2,1)}, u32[]{:S(2)}) copy-start(bf16[512,1024]{1,0:T(8,128)(2,1)} %param.12) | copy-start | bytes 3145732
  7.2 109.1 %all-reduce.3.cloned.1.call-start = ((), (), s32[]{:S(2)}) async-start(), calls=%async_computation.2 | async-start | bytes 2097152 | tf_op jit(solution)/shard_map/psum | solution.py:66
  8.0 17.7 %copy-start.28 = (bf16[1,256,512]{2,1,0:T(8,128)(2,1)S(1)}, bf16[1,256,512]{2,1,0:T(8,128)(2,1)}, u32[]{:S(2)}) copy-start(bf16[1,256,512]{2,1,0:T(8,128)(2,1)} %param.8) | copy-start | bytes 786436
  26.6 33.7 %copy-start.1 = (f32[512,256]{0,1:T(8,128)}, f32[512,256]{0,1:T(8,128)S(1)}, u32[]{:S(2)}) copy-start(f32[512,256]{0,1:T(8,128)S(1)} %get-tuple-element.61) | copy-start | bytes 1572868
  30.9 20.6 %copy-start.30 = (bf16[1,256,512]{2,1,0:T(8,128)(2,1)S(1)}, bf16[1,256,512]{2,1,0:T(8,128)(2,1)}, u32[]{:S(2)}) copy-start(bf16[1,256,512]{2,1,0:T(8,128)(2,1)} %param.9) | copy-start | bytes 786436
  51.5 2.0 %copy-start.13 = (f32[512,256]{0,1:T(8,128)S(1)}, f32[512,256]{0,1:T(8,128)}, u32[]{:S(2)}) copy-start(f32[512,256]{0,1:T(8,128)} %get-tuple-element.53) | copy-start | bytes 1572868
  53.6 1.0 copy-start.10
  54.5 1.1 copy-start.7
  55.5 1.1 copy-start.4
  60.3 89.7 %reduce-scatter.7.cloned.1.call-start = ((), (), s32[]{:S(2)}) async-start(), calls=%async_computation.5 | async-start | bytes 655360
  105.6 2.0 %copy-start.14 = (f32[512,256]{0,1:T(8,128)S(1)}, f32[512,256]{0,1:T(8,128)}, u32[]{:S(2)}) copy-start(f32[512,256]{0,1:T(8,128)} %get-tuple-element.53) | copy-start | bytes 1572868
  107.6 1.0 copy-start.11
  108.7 1.0 copy-start.8
  109.7 1.0 copy-start.5
  110.7 1.0 copy-start.2
  116.3 2.3 %copy-start.32 = (f32[512,256]{0,1:T(8,128)S(1)}, f32[512,256]{0,1:T(8,128)}, u32[]{:S(2)}) copy-start(f32[512,256]{0,1:T(8,128)} %get-tuple-element.51) | copy-start | bytes 1572868
  118.6 1.0 copy-start.15
  118.9 6.5 %copy-start.20 = (bf16[512,256]{0,1:T(8,128)(2,1)}, bf16[512,256]{0,1:T(8,128)(2,1)S(1)}, u32[]{:S(2)}) copy-start(bf16[512,256]{0,1:T(8,128)(2,1)S(1)} %fusion.31) | copy-start | bytes 786436
  119.7 1.0 copy-start.12
  120.0 6.3 %copy-start.22 = (bf16[512,256]{0,1:T(8,128)(2,1)}, bf16[512,256]{0,1:T(8,128)(2,1)S(1)}, u32[]{:S(2)}) copy-start(bf16[512,256]{0,1:T(8,128)(2,1)S(1)} %fusion.30) | copy-start | bytes 786436
  120.7 1.0 copy-start.9
  121.0 5.6 %copy-start.24 = (bf16[512,256]{0,1:T(8,128)(2,1)}, bf16[512,256]{0,1:T(8,128)(2,1)S(1)}, u32[]{:S(2)}) copy-start(bf16[512,256]{0,1:T(8,128)(2,1)S(1)} %fusion.29) | copy-start | bytes 786436
  121.8 1.0 copy-start.6
  122.1 4.7 %copy-start.26 = (bf16[512,256]{0,1:T(8,128)(2,1)}, bf16[512,256]{0,1:T(8,128)(2,1)S(1)}, u32[]{:S(2)}) copy-start(bf16[512,256]{0,1:T(8,128)(2,1)S(1)} %fusion.28) | copy-start | bytes 786436
  122.8 1.0 copy-start.3
  123.0 4.0 %copy-start.18 = (bf16[512,256]{0,1:T(8,128)(2,1)}, bf16[512,256]{0,1:T(8,128)(2,1)S(1)}, u32[]{:S(2)}) copy-start(bf16[512,256]{0,1:T(8,128)(2,1)S(1)} %fusion.27) | copy-start | bytes 786436
  123.8 0.9 copy-start.31
  124.1 3.1 %copy-start.16 = (bf16[512,256]{0,1:T(8,128)(2,1)}, bf16[512,256]{0,1:T(8,128)(2,1)S(1)}, u32[]{:S(2)}) copy-start(bf16[512,256]{0,1:T(8,128)(2,1)S(1)} %fusion.26) | copy-start | bytes 786436
  125.1 1.0 copy-start.29
  129.1 0.9 copy-start.21
  129.1 1.1 copy-start.23
  129.1 43.6 %all-reduce.5.cloned.1.call-start = ((), (), s32[]{:S(2)}) async-start(), calls=%async_computation.4 | async-start | bytes 262144 | tf_op jit(solution)/shard_map/psum | solution.py:124
  130.2 1.0 copy-start.25
  131.2 0.9 copy-start.27
  132.4 0.7 copy-start.33
  133.1 18.6 %copy-start.34 = (bf16[1,256,512]{1,2,0:T(8,128)(2,1)S(1)}, bf16[1,256,512]{1,2,0:T(8,128)(2,1)}, u32[]{:S(2)}) copy-start(bf16[1,256,512]{1,2,0:T(8,128)(2,1)} %copy-done.33) | copy-start | bytes 786436
  135.1 16.7 %copy-start.19 = (bf16[512,256]{0,1:T(8,128)(2,1)S(1)}, bf16[512,256]{0,1:T(8,128)(2,1)}, u32[]{:S(2)}) copy-start(bf16[512,256]{0,1:T(8,128)(2,1)} %copy-done.18) | copy-start | bytes 786436
  151.7 1.0 copy-start.17
  151.7 31.4 %reduce-scatter.5.cloned.1.call-start = ((), (), s32[]{:S(2)}) async-start(), calls=%async_computation.3 | async-start | bytes 393216 | tf_op jit(solution)/shard_map/reduce_scatter | solution.py:76
Sparse Core Ops, SparseCore 0:
  60.4 55.5 all-reduce.2
  129.2 20.7 reduce-scatter.6
  152.9 19.6 all-reduce.4
  175.4 7.6 reduce-scatter.4
where the time goes:
time: 191 us; the launch traced here: 190 us
  blocking collectives  77.8 us (41%)
  waiting for transfers between devices  42.4 us (22%)
  matrix products  32.4 us (17%)
  local copies, waits for them, and re-layouts  16.6 us (9%)
  between operations  14.8 us (8%)
  other arithmetic  5.53 us (3%)
    all_gather x1, blocking collectives, body(): upstream_all = lax.all_gather(upstream, 'seq', axis=0, tiled=True)  20.8 us
    psum x1, blocking collectives, body(): weighted, totals = lax.psum((partial_sums, partial_totals), 'seq')  19.9 us
    pmax x1, blocking collectives, body(): row_top = lax.pmax(local_top, 'seq')  19.5 us
    psum x1, waiting for transfers between devices, body(): grad_latents = lax.psum(own_grad, 'slide').astype(jnp.float32)  18.4 us
    all_gather x1, blocking collectives, body(): queries = lax.all_gather(latents, 'seq', axis=0, tiled=True)  17.7 us
    unnamed x75, local copies, waits for them, and re-layouts  16.4 us
    unnamed x5, waiting for transfers between devices  15.2 us
    reduce_scatter x1, waiting for transfers between devices, body(): lax.psum_scatter(pooled_part.astype(jnp.bfloat16), 'head', scatter_dimens...  8.73 us
  transfers between devices with their start and end apart: 4, of which 3 were waited for; matrix products, arithmetic and copies ran while one was open for 11% of the time, Pallas kernels for 0%

commit v1 on v0

--- a/solution.py
+++ b/solution.py
@@ -1,6 +1,10 @@
+import functools
+
 import jax
 import jax.numpy as jnp
 from jax import lax
+from jax.experimental import pallas as pl
+from jax.experimental.pallas import tpu as pltpu
 from jax.sharding import PartitionSpec as P
 
 HD = 64
@@ -8,6 +12,350 @@
 
 
 masked_score = -1e30
+
+
+MESH = pl.DeviceIdType.MESH
+
+
+def dot(a, b, dims):
+    return lax.dot_general(a, b, (dims, ((), ())), preferred_element_type=jnp.float32)
+
+
+def swap_kernel(
+    n,
+    slides,
+    latents,
+    keys,
+    values,
+    mask,
+    count,
+    weight,
+    cot,
+    pooled,
+    grad_latents,
+    grad_keys,
+    grad_values,
+    q_all,
+    k_all,
+    v_all,
+    u_all,
+    mask_own,
+    mask_all,
+    w_buf,
+    cot_buf,
+    u_own,
+    probs,
+    att,
+    att_in,
+    part_out,
+    part_in,
+    gk,
+    gv,
+    gq,
+    gq_in,
+    gq_sum,
+    gl_in,
+    local_sem,
+    send_sem,
+    recv_sem,
+    slide_send,
+    slide_recv,
+    head_send,
+    head_recv,
+):
+    me = lax.axis_index("seq")
+    my_head = lax.axis_index("head")
+    my_slide = lax.axis_index("slide")
+    rows = latents.shape[0]
+    tiles = keys.shape[1]
+    blk = q_all.shape[1]
+    heads = blk // HD
+    width = latents.shape[1]
+    all_rows = n * rows
+    blocks = tiles // BLOCK
+    factor = HD ** (-0.5)
+
+    def cols(j):
+        return pl.ds(pl.multiple_of(j * blk, 128), blk)
+
+    def rows_of(j, size):
+        return pl.ds(pl.multiple_of(j * size, 128), size)
+
+    def peer(d):
+        return lax.rem(me + d, n)
+
+    barrier = pltpu.get_barrier_semaphore()
+    for d in range(1, n):
+        pl.semaphore_signal(barrier, inc=1, device_id={"seq": peer(d)}, device_id_type=MESH)
+    for e in range(1, slides):
+        other = lax.rem(my_slide + e, slides)
+        pl.semaphore_signal(barrier, inc=1, device_id={"slide": other}, device_id_type=MESH)
+    pl.semaphore_signal(barrier, inc=1, device_id={"head": 1 - my_head}, device_id_type=MESH)
+
+    def local(src, dst, i):
+        copy = pltpu.make_async_copy(src, dst, local_sem.at[i])
+        copy.start()
+        return copy
+
+    w_copy = local(weight, w_buf, 0)
+    cot_copy = local(cot.at[0], cot_buf, 1)
+    own_q = local(latents.at[:, cols(me)], q_all.at[rows_of(me, rows)], 2)
+    own_k = local(keys.at[0, :, cols(me)], k_all.at[rows_of(me, tiles)], 3)
+    own_v = local(values.at[0, :, cols(me)], v_all.at[rows_of(me, tiles)], 4)
+    mask_own[...] = jnp.zeros_like(mask_own)
+    for b in range(blocks):
+        mask_own[pl.ds(b, 1), :] = jnp.full((1, 128), mask[0, b], jnp.int32)
+    mask_all[me] = mask_own[...]
+
+    sent = []
+
+    def send(kind, d, src, dst):
+        copy = pltpu.make_async_remote_copy(
+            src_ref=src,
+            dst_ref=dst,
+            send_sem=send_sem.at[kind, d - 1],
+            recv_sem=recv_sem.at[kind, d - 1],
+            device_id={"seq": peer(d)},
+            device_id_type=MESH,
+        )
+        copy.start()
+        sent.append(copy)
+        return copy
+
+    far = list(range(1, n))
+    pl.semaphore_wait(barrier, n - 1 + slides - 1 + 1)
+    mask_moves = [send(0, d, mask_own, mask_all.at[me]) for d in far]
+    q_moves = [send(1, d, latents.at[:, cols(peer(d))], q_all.at[rows_of(me, rows)]) for d in far]
+    k_moves = [send(2, d, keys.at[0, :, cols(peer(d))], k_all.at[rows_of(me, tiles)]) for d in far]
+    v_moves = [send(3, d, values.at[0, :, cols(peer(d))], v_all.at[rows_of(me, tiles)]) for d in far]
+
+    live_count = count[0]
+    w_copy.wait()
+    cot_copy.wait()
+    own_row = lax.broadcasted_iota(jnp.int32, (rows, 1), 0) + me * rows
+    for j in range(n):
+        projected = dot(cot_buf[...], w_buf[j * blk : (j + 1) * blk, :], ((1,), (1,)))
+        u_own[:, j * blk : (j + 1) * blk] = jnp.where(own_row < live_count, projected, 0.0).astype(
+            jnp.bfloat16
+        )
+    own_u = local(u_own.at[:, cols(me)], u_all.at[rows_of(me, rows)], 5)
+    u_moves = [send(4, d, u_own.at[:, cols(peer(d))], u_all.at[rows_of(me, rows)]) for d in far]
+
+    lane = lax.broadcasted_iota(jnp.int32, (1, blk), 1) // HD
+
+    def only(x, h):
+        return jnp.where(lane == h, x, jnp.zeros_like(x))
+
+    own_q.wait()
+    own_k.wait()
+    for copy in mask_moves + q_moves + k_moves:
+        copy.wait_recv()
+
+    tops = []
+    totals = []
+    for h in range(heads):
+        query = only(q_all[...], h)
+
+        def score_step(i, top, h=h, query=query):
+            for b in range(blocks):
+                at = pl.ds(pl.multiple_of(i * tiles + b * BLOCK, BLOCK), BLOCK)
+                score = dot(k_all[at, :], query, ((1,), (1,))) * factor
+                valid = jnp.broadcast_to(mask_all[i][b : b + 1, :1], (1, all_rows)) > 0
+                score = jnp.where(valid, score, masked_score)
+                probs[h, at, :] = score
+                top = jnp.maximum(top, jnp.max(score, axis=0, keepdims=True))
+            return top
+
+        top = lax.fori_loop(0, n, score_step, jnp.full((1, all_rows), masked_score, jnp.float32))
+
+        def exp_step(i, total, h=h, top=top):
+            for b in range(blocks):
+                at = pl.ds(pl.multiple_of(i * tiles + b * BLOCK, BLOCK), BLOCK)
+                expos = jnp.exp(probs[h, at, :] - top)
+                probs[h, at, :] = expos
+                total = total + jnp.sum(expos, axis=0, keepdims=True)
+            return total
+
+        totals.append(lax.fori_loop(0, n, exp_step, jnp.zeros((1, all_rows), jnp.float32)))
+    inverse = [1.0 / total for total in totals]
+
+    own_v.wait()
+    for copy in v_moves:
+        copy.wait_recv()
+
+    def attend_step(i, sums):
+        at = rows_of(i, tiles)
+        v_block = v_all[at, :]
+        return tuple(
+            sums[h] + dot(only(v_block, h), probs[h, at, :].astype(jnp.bfloat16), ((0,), (0,)))
+            for h in range(heads)
+        )
+
+    zero = jnp.zeros((blk, all_rows), jnp.float32)
+    sums = lax.fori_loop(0, n, attend_step, (zero,) * heads)
+    attended = sums[0] * inverse[0]
+    for h in range(1, heads):
+        attended = attended + sums[h] * inverse[h]
+    every_row = lax.broadcasted_iota(jnp.int32, (1, all_rows), 1)
+    attended = jnp.where(every_row < live_count, attended, 0.0)
+    attended_rows = attended.T.astype(jnp.bfloat16)
+    att[...] = attended_rows
+    own_att = local(att.at[rows_of(me, rows)], att_in.at[:, cols(me)], 6)
+    att_moves = [send(5, d, att.at[rows_of(peer(d), rows)], att_in.at[:, cols(me)]) for d in far]
+
+    own_u.wait()
+    for copy in u_moves:
+        copy.wait_recv()
+    product = u_all[...].astype(jnp.float32) * attended_rows.astype(jnp.float32)
+    product = product.T
+    delta = [jnp.sum(product[h * HD : (h + 1) * HD], axis=0, keepdims=True) for h in range(heads)]
+
+    grad_q = zero
+    gk_moves = []
+    gv_moves = []
+    for d in far[::-1] + [0]:
+        j = peer(d)
+        at = rows_of(j, tiles)
+        v_block = v_all[at, :]
+        k_block = k_all[at, :]
+        grad_k = grad_v = None
+        for h in range(heads):
+            query = only(q_all[...], h)
+            up = only(u_all[...], h)
+            grad_prob = dot(v_block, up, ((1,), (1,)))
+            weights = probs[h, at, :] * inverse[h]
+            grad_score = (weights * (grad_prob - delta[h]) * factor).astype(jnp.bfloat16)
+            more_v = dot(weights.astype(jnp.bfloat16), up, ((1,), (0,)))
+            more_k = dot(grad_score, query, ((1,), (0,)))
+            grad_v = more_v if grad_v is None else grad_v + more_v
+            grad_k = more_k if grad_k is None else grad_k + more_k
+            grad_q = grad_q + dot(only(k_block, h), grad_score, ((0,), (0,)))
+        gk[at, :] = grad_k.astype(jnp.bfloat16)
+        gv[at, :] = grad_v.astype(jnp.bfloat16)
+        if d:
+            gk_moves.append(send(6, d, gk.at[at], grad_keys.at[0, :, cols(me)]))
+            gv_moves.append(send(7, d, gv.at[at], grad_values.at[0, :, cols(me)]))
+        else:
+            own_gk = local(gk.at[at], grad_keys.at[0, :, cols(me)], 7)
+            own_gv = local(gv.at[at], grad_values.at[0, :, cols(me)], 8)
+
+    grad_rows = grad_q.T
+    gq[...] = grad_rows.astype(jnp.bfloat16)
+    slide_moves = []
+    for e in range(1, slides):
+        copy = pltpu.make_async_remote_copy(
+            src_ref=gq,
+            dst_ref=gq_in.at[e - 1],
+            send_sem=slide_send.at[e - 1],
+            recv_sem=slide_recv.at[e - 1],
+            device_id={"slide": lax.rem(my_slide + e, slides)},
+            device_id_type=MESH,
+        )
+        copy.start()
+        slide_moves.append(copy)
+
+    own_att.wait()
+    for copy in att_moves:
+        copy.wait_recv()
+    half = pooled.shape[2]
+    mine = pl.ds(pl.multiple_of(my_head * half, 128), half)
+    theirs = pl.ds(pl.multiple_of((1 - my_head) * half, 128), half)
+    part_out[...] = dot(att_in[...], w_buf[:, theirs], ((1,), (0,))).astype(jnp.bfloat16)
+    head_move = pltpu.make_async_remote_copy(
+        src_ref=part_out,
+        dst_ref=part_in,
+        send_sem=head_send,
+        recv_sem=head_recv,
+        device_id={"head": 1 - my_head},
+        device_id_type=MESH,
+    )
+    head_move.start()
+    own_part = dot(att_in[...], w_buf[:, mine], ((1,), (0,)))
+
+    total = grad_rows
+    for e, copy in enumerate(slide_moves):
+        copy.wait_recv()
+        total = total + gq_in[e].astype(jnp.float32)
+    gq_sum[...] = total.astype(jnp.bfloat16)
+    own_gl = local(gq_sum.at[rows_of(me, rows)], gl_in.at[:, cols(me)], 9)
+    gl_moves = [send(8, d, gq_sum.at[rows_of(peer(d), rows)], gl_in.at[:, cols(me)]) for d in far]
+
+    head_move.wait_recv()
+    pooled[0] = (own_part + part_in[...].astype(jnp.float32)).astype(jnp.bfloat16)
+
+    own_gl.wait()
+    for copy in gl_moves:
+        copy.wait_recv()
+    grad_latents[...] = gl_in[...].astype(jnp.float32)
+    own_gk.wait()
+    own_gv.wait()
+    for copy in gk_moves + gv_moves:
+        copy.wait_recv()
+    for copy in sent + slide_moves + [head_move]:
+        copy.wait_send()
+
+
+def swapped_body(latents, tile_keys, tile_values, tile_mask, latent_counts, out_weight, cotangent):
+    n = lax.axis_size("seq")
+    slides = lax.axis_size("slide")
+    rows, width = latents.shape
+    tiles = tile_keys.shape[1]
+    depth = out_weight.shape[1]
+    blk = width // n
+    heads = blk // HD
+    half = depth // 2
+    bf16 = jnp.bfloat16
+    anywhere = pl.BlockSpec(memory_space=pl.ANY)
+    scalars = pl.BlockSpec(memory_space=pltpu.SMEM)
+    vmem = pl.BlockSpec(memory_space=pltpu.VMEM)
+    dma = pltpu.SemaphoreType.DMA
+    flops = 2 * heads * 6 * n * rows * n * tiles * HD + 4 * rows * width * depth
+    return pl.pallas_call(
+        functools.partial(swap_kernel, n, slides),
+        out_shape=(
+            jax.ShapeDtypeStruct((1, rows, half), bf16),
+            jax.ShapeDtypeStruct((rows, width), jnp.float32),
+            jax.ShapeDtypeStruct(tile_keys.shape, bf16),
+            jax.ShapeDtypeStruct(tile_values.shape, bf16),
+        ),
+        in_specs=[anywhere, anywhere, anywhere, scalars, scalars, anywhere, anywhere],
+        out_specs=(vmem, vmem, anywhere, anywhere),
+        scratch_shapes=[
+            pltpu.VMEM((n * rows, blk), bf16),
+            pltpu.VMEM((n * tiles, blk), bf16),
+            pltpu.VMEM((n * tiles, blk), bf16),
+            pltpu.VMEM((n * rows, blk), bf16),
+            pltpu.VMEM((8 * pl.cdiv(tiles // BLOCK, 8), 128), jnp.int32),
+            pltpu.VMEM((n, 8 * pl.cdiv(tiles // BLOCK, 8), 128), jnp.int32),
+            pltpu.VMEM((width, depth), bf16),
+            pltpu.VMEM((rows, depth), bf16),
+            pltpu.VMEM((rows, width), bf16),
+            pltpu.VMEM((heads, n * tiles, n * rows), jnp.float32),
+            pltpu.VMEM((n * rows, blk), bf16),
+            pltpu.VMEM((rows, width), bf16),
+            pltpu.VMEM((rows, half), bf16),
+            pltpu.VMEM((rows, half), bf16),
+            pltpu.VMEM((n * tiles, blk), bf16),
+            pltpu.VMEM((n * tiles, blk), bf16),
+            pltpu.VMEM((n * rows, blk), bf16),
+            pltpu.VMEM((slides - 1, n * rows, blk), bf16),
+            pltpu.VMEM((n * rows, blk), bf16),
+            pltpu.VMEM((rows, width), bf16),
+            dma((10,)),
+            dma((9, n - 1)),
+            dma((9, n - 1)),
+            dma((slides - 1,)),
+            dma((slides - 1,)),
+            dma,
+            dma,
+        ],
+        compiler_params=pltpu.CompilerParams(
+            collective_id=0, has_side_effects=True, vmem_limit_bytes=40 * 1024 * 1024
+        ),
+        cost_estimate=pl.CostEstimate(
+            flops=flops, bytes_accessed=8 * rows * depth * 2, transcendentals=heads * n * rows * n * tiles
+        ),
+    )(latents, tile_keys, tile_values, tile_mask, latent_counts, out_weight, cotangent)
 
 
 def body(latents, tile_keys, tile_values, tile_mask, latent_counts, out_weight, cotangent):
@@ -140,8 +488,16 @@
         P("head", None),
         P(("groups", "slide"), "seq", None),
     )
+    block_width = 128 * mesh.shape["seq"]
+    swapped = mesh.shape["seq"] > 1 and mesh.shape["slide"] > 1 and mesh.shape["head"] == 2
+
+    def chosen(latents, *others):
+        by_heads = swapped and latents.shape[1] % block_width == 0
+        by_heads = by_heads and latents.shape[0] % 128 == 0 and others[0].shape[1] % BLOCK == 0
+        return (swapped_body if by_heads else body)(latents, *others)
+
     return jax.shard_map(
-        body,
+        chosen,
         mesh=mesh,
         in_specs=placed,
         out_specs=(

time: 191 us -> 50.9 us (0.27)
  blocking collectives: 77.8 us -> 0 us
  waiting for transfers between devices: 42.4 us -> 0 us
  Pallas kernels: 0 us -> 41.6 us
  matrix products: 32.4 us -> 0 us
  between operations: 14.8 us -> 1.33 us
  local copies, waits for them, and re-layouts: 16.6 us -> 7.74 us
  other arithmetic: 5.53 us -> 0 us
    pallas_call x0 -> x1, Pallas kernels: none -> 41.6 us  [swapped_body(): pl.pallas_call(functools.partial(swap_kernel, n, slides), out_shape=(jax....]
    all_gather x2 -> x0, blocking collectives: 38.5 us -> none  [the longest x1 20.8 us: body(): upstream_all = lax.all_gather(upstream, 'seq', axis=0, tiled=True)]
    dot_general x50 -> x0, matrix products: 32.4 us -> none  [the longest x8 8.47 us: body(): jnp.dot(expos.astype(jnp.bfloat16), value_block[:, columns], preferred_el...]
    psum x1 -> x0, blocking collectives: 19.9 us -> none  [body(): weighted, totals = lax.psum((partial_sums, partial_totals), 'seq')]
    pmax x1 -> x0, blocking collectives: 19.5 us -> none  [body(): row_top = lax.pmax(local_top, 'seq')]
    psum x2 -> x0, waiting for transfers between devices: 18.4 us -> none  [the longest x1 18.4 us: body(): grad_latents = lax.psum(own_grad, 'slide').astype(jnp.float32)]
    unnamed x5 -> x0, waiting for transfers between devices: 15.2 us -> none
    reduce_scatter x1 -> x0, waiting for transfers between devices: 8.73 us -> none  [body(): lax.psum_scatter(pooled_part.astype(jnp.bfloat16), 'head', scatter_dimens...]
  transfers between devices with their start and end apart: 4 -> 0, of which waited for: 3 -> 0; matrix products, arithmetic and copies ran while one was open for 11% -> 0% of each run, Pallas kernels for 0% -> 0%
where the time goes in v1:
time: 50.9 us; the launch traced here: 50.7 us
  Pallas kernels  41.6 us (82%)
  local copies, waits for them, and re-layouts  7.74 us (15%)
  between operations  1.33 us (3%)
    pallas_call x1, Pallas kernels, swapped_body(): pl.pallas_call(functools.partial(swap_kernel, n, slides), out_shape=(jax....  41.6 us
    unnamed x16, local copies, waits for them, and re-layouts  7.74 us

profile of v1, /device:TPU:0, one launch (start us, length us, event | category | flops | bytes accessed | tf_op | source)
XLA Modules:
  0.0 50.7 jit_solution(6192670052166379080)
XLA Ops:
  0.6 0.0 copy-start.5
  1.3 0.0 copy-done.5
  1.3 0.0 copy-start
  1.3 1.2 %copy-done = bf16[512,1024]{1,0:T(8,128)(2,1)S(1)} copy-done((bf16[512,1024]{1,0:T(8,128)(2,1)S(1)}, bf16[512,1024]{1,0:T(8,128)(2,1)}, u32[]{:S(2)}) %copy-start) | copy-done | bytes 1048600
  2.5 0.0 copy-start.1
  2.5 0.9 %copy-done.1 = bf16[1,256,512]{2,1,0:T(8,128)(2,1)S(1)} copy-done((bf16[1,256,512]{2,1,0:T(8,128)(2,1)S(1)}, bf16[1,256,512]{2,1,0:T(8,128)(2,1)}, u32[]{:S(2)}) %copy-start.1) | copy-done | bytes 262168
  3.5 0.0 copy-start.2
  3.5 0.9 %copy-done.2 = bf16[1,256,512]{2,1,0:T(8,128)(2,1)S(1)} copy-done((bf16[1,256,512]{2,1,0:T(8,128)(2,1)S(1)}, bf16[1,256,512]{2,1,0:T(8,128)(2,1)}, u32[]{:S(2)}) %copy-start.2) | copy-done | bytes 262168
  4.4 0.0 copy-start.3
  4.4 0.9 %copy-done.3 = bf16[1,128,1024]{2,1,0:T(8,128)(2,1)S(1)} copy-done((bf16[1,128,1024]{2,1,0:T(8,128)(2,1)S(1)}, bf16[1,128,1024]{2,1,0:T(8,128)(2,1)}, u32[]{:S(2)}) %copy-start.3) | copy-done | bytes 262168
  5.4 0.0 copy-start.4
  5.4 0.9 %copy-done.4 = bf16[128,512]{1,0:T(8,128)(2,1)S(1)} copy-done((bf16[128,512]{1,0:T(8,128)(2,1)S(1)}, bf16[128,512]{1,0:T(8,128)(2,1)}, u32[]{:S(2)}) %copy-start.4) | copy-done | bytes 131096
  6.3 41.6 %shard_map.102 = (bf16[1,128,512]{2,1,0:T(8,128)(2,1)S(1)}, f32[128,512]{1,0:T(8,128)S(1)}, bf16[1,256,512]{2,1,0:T(8,128)(2,1)S(1)}, bf16[1,256,512]{2,1,0:T(8,128)(2,1)S(1)}) custom-call(bf16[128,512]{1,0:T(8,128)(2,1)S(1)} %copy-done.4, bf16[1,256,512]{2,1,0:T(8,128)(2,1)S(1)} %copy-done.1, bf16[1,256,512]{2,1,0:T(8,128)(2,1)S(1)} %copy-done.2, ...), custom_call_target="tpu_custom_call" | custom-call | flops 1073741824 | bytes 2097152 | tf_op jit(solution)/shard_map/pallas_call | solution.py:313
  47.9 0.7 %copy.16 = bf16[1,128,512]{2,1,0:T(8,128)(2,1)} copy(bf16[1,128,512]{2,1,0:T(8,128)(2,1)S(1)} %get-tuple-element.8) | data formatting | bytes 262144
  48.6 0.7 %copy.17 = f32[128,512]{1,0:T(8,128)} copy(f32[128,512]{1,0:T(8,128)S(1)} %get-tuple-element.9) | data formatting | bytes 524288
  49.3 0.7 %copy.18 = bf16[1,256,512]{2,1,0:T(8,128)(2,1)} copy(bf16[1,256,512]{2,1,0:T(8,128)(2,1)S(1)} %get-tuple-element.10) | data formatting | bytes 524288
  50.0 0.7 %copy.19 = bf16[1,256,512]{2,1,0:T(8,128)(2,1)} copy(bf16[1,256,512]{2,1,0:T(8,128)(2,1)S(1)} %get-tuple-element.11) | data formatting | bytes 524288
Async XLA Ops:
  0.6 0.7 %copy-start.5 = (s32[1,2]{1,0:T(1,128)S(1)}, s32[1,2]{1,0:T(1,128)}, u32[]{:S(2)}) copy-start(s32[1,2]{1,0:T(1,128)} %mask.1) | copy-start | bytes 28
  1.3 1.2 %copy-start = (bf16[512,1024]{1,0:T(8,128)(2,1)S(1)}, bf16[512,1024]{1,0:T(8,128)(2,1)}, u32[]{:S(2)}) copy-start(bf16[512,1024]{1,0:T(8,128)(2,1)} %weight.1) | copy-start | bytes 3145732
  2.5 0.9 %copy-start.1 = (bf16[1,256,512]{2,1,0:T(8,128)(2,1)S(1)}, bf16[1,256,512]{2,1,0:T(8,128)(2,1)}, u32[]{:S(2)}) copy-start(bf16[1,256,512]{2,1,0:T(8,128)(2,1)} %keys.1) | copy-start | bytes 786436
  3.5 0.9 %copy-start.2 = (bf16[1,256,512]{2,1,0:T(8,128)(2,1)S(1)}, bf16[1,256,512]{2,1,0:T(8,128)(2,1)}, u32[]{:S(2)}) copy-start(bf16[1,256,512]{2,1,0:T(8,128)(2,1)} %values.1) | copy-start | bytes 786436
  4.4 0.9 %copy-start.3 = (bf16[1,128,1024]{2,1,0:T(8,128)(2,1)S(1)}, bf16[1,128,1024]{2,1,0:T(8,128)(2,1)}, u32[]{:S(2)}) copy-start(bf16[1,128,1024]{2,1,0:T(8,128)(2,1)} %cot.1) | copy-start | bytes 786436
  5.4 0.9 %copy-start.4 = (bf16[128,512]{1,0:T(8,128)(2,1)S(1)}, bf16[128,512]{1,0:T(8,128)(2,1)}, u32[]{:S(2)}) copy-start(bf16[128,512]{1,0:T(8,128)(2,1)} %latents.1) | copy-start | bytes 393220

commit v2 on v1

--- a/solution.py
+++ b/solution.py
@@ -55,11 +55,15 @@
     gq_in,
     gq_sum,
     gl_in,
+    pooled_buf,
+    gl_buf,
     local_sem,
     send_sem,
     recv_sem,
     slide_send,
     slide_recv,
+    share_send,
+    share_recv,
     head_send,
     head_recv,
 ):
@@ -68,7 +72,8 @@
     my_slide = lax.axis_index("slide")
     rows = latents.shape[0]
     tiles = keys.shape[1]
-    blk = q_all.shape[1]
+    blk = k_all.shape[1]
+    share = rows // slides
     heads = blk // HD
     width = latents.shape[1]
     all_rows = n * rows
@@ -82,7 +87,12 @@
         return pl.ds(pl.multiple_of(j * size, 128), size)
 
     def peer(d):
-        return lax.rem(me + d, n)
+        other, bit = me, 1
+        while bit < n:
+            if d & bit:
+                other = other + bit - 2 * bit * lax.rem(lax.div(me, bit), 2)
+            bit *= 2
+        return other
 
     barrier = pltpu.get_barrier_semaphore()
     for d in range(1, n):
@@ -99,7 +109,8 @@
 
     w_copy = local(weight, w_buf, 0)
     cot_copy = local(cot.at[0], cot_buf, 1)
-    own_q = local(latents.at[:, cols(me)], q_all.at[rows_of(me, rows)], 2)
+    my_share = pl.ds(pl.multiple_of(my_slide * share, 16), share)
+    own_q = local(latents.at[my_share, cols(me)], q_all.at[me, my_slide], 2)
     own_k = local(keys.at[0, :, cols(me)], k_all.at[rows_of(me, tiles)], 3)
     own_v = local(values.at[0, :, cols(me)], v_all.at[rows_of(me, tiles)], 4)
     mask_own[...] = jnp.zeros_like(mask_own)
@@ -122,39 +133,52 @@
         sent.append(copy)
         return copy
 
-    far = list(range(1, n))
+    far = [n // 2] + [d for d in range(n - 1, 0, -1) if d != n // 2]
     pl.semaphore_wait(barrier, n - 1 + slides - 1 + 1)
     mask_moves = [send(0, d, mask_own, mask_all.at[me]) for d in far]
-    q_moves = [send(1, d, latents.at[:, cols(peer(d))], q_all.at[rows_of(me, rows)]) for d in far]
+    q_moves = [send(1, d, latents.at[my_share, cols(peer(d))], q_all.at[me, my_slide]) for d in far]
     k_moves = [send(2, d, keys.at[0, :, cols(peer(d))], k_all.at[rows_of(me, tiles)]) for d in far]
-    v_moves = [send(3, d, values.at[0, :, cols(peer(d))], v_all.at[rows_of(me, tiles)]) for d in far]
 
     live_count = count[0]
     w_copy.wait()
     cot_copy.wait()
     own_row = lax.broadcasted_iota(jnp.int32, (rows, 1), 0) + me * rows
-    for j in range(n):
-        projected = dot(cot_buf[...], w_buf[j * blk : (j + 1) * blk, :], ((1,), (1,)))
-        u_own[:, j * blk : (j + 1) * blk] = jnp.where(own_row < live_count, projected, 0.0).astype(
-            jnp.bfloat16
-        )
+    projected = dot(cot_buf[...], w_buf[...], ((1,), (1,)))
+    u_own[...] = jnp.where(own_row < live_count, projected, 0.0).astype(jnp.bfloat16)
     own_u = local(u_own.at[:, cols(me)], u_all.at[rows_of(me, rows)], 5)
     u_moves = [send(4, d, u_own.at[:, cols(peer(d))], u_all.at[rows_of(me, rows)]) for d in far]
 
+    v_moves = [send(3, d, values.at[0, :, cols(peer(d))], v_all.at[rows_of(me, tiles)]) for d in far]
+
     lane = lax.broadcasted_iota(jnp.int32, (1, blk), 1) // HD
 
     def only(x, h):
         return jnp.where(lane == h, x, jnp.zeros_like(x))
 
     own_q.wait()
+    for copy in q_moves:
+        copy.wait_recv()
+    share_moves = []
+    for e in range(1, slides):
+        copy = pltpu.make_async_remote_copy(
+            src_ref=q_all.at[:, my_slide],
+            dst_ref=q_all.at[:, my_slide],
+            send_sem=share_send.at[e - 1],
+            recv_sem=share_recv.at[e - 1],
+            device_id={"slide": lax.rem(my_slide + e, slides)},
+            device_id_type=MESH,
+        )
+        copy.start()
+        share_moves.append(copy)
     own_k.wait()
-    for copy in mask_moves + q_moves + k_moves:
-        copy.wait_recv()
+    for copy in mask_moves + share_moves + k_moves:
+        copy.wait_recv()
+    q_rows = q_all[...].reshape(all_rows, blk)
 
     tops = []
     totals = []
     for h in range(heads):
-        query = only(q_all[...], h)
+        query = only(q_rows, h)
 
         def score_step(i, top, h=h, query=query):
             for b in range(blocks):
@@ -179,6 +203,26 @@
         totals.append(lax.fori_loop(0, n, exp_step, jnp.zeros((1, all_rows), jnp.float32)))
     inverse = [1.0 / total for total in totals]
 
+    own_u.wait()
+    for copy in u_moves:
+        copy.wait_recv()
+    u_rows = u_all[...]
+    gv_moves = []
+    for d in far + [0]:
+        j = peer(d)
+        at = rows_of(j, tiles)
+        grad_v = None
+        for h in range(heads):
+            weights = probs[h, at, :] * inverse[h]
+            probs[h, at, :] = weights
+            more_v = dot(weights.astype(jnp.bfloat16), only(u_rows, h), ((1,), (0,)))
+            grad_v = more_v if grad_v is None else grad_v + more_v
+        gv[at, :] = grad_v.astype(jnp.bfloat16)
+        if d:
+            gv_moves.append(send(7, d, gv.at[at], grad_values.at[0, :, cols(me)]))
+        else:
+            own_gv = local(gv.at[at], grad_values.at[0, :, cols(me)], 8)
+
     own_v.wait()
     for copy in v_moves:
         copy.wait_recv()
@@ -186,16 +230,13 @@
     def attend_step(i, sums):
         at = rows_of(i, tiles)
         v_block = v_all[at, :]
-        return tuple(
-            sums[h] + dot(only(v_block, h), probs[h, at, :].astype(jnp.bfloat16), ((0,), (0,)))
-            for h in range(heads)
-        )
+        for h in range(heads):
+            weights = probs[h, at, :].astype(jnp.bfloat16)
+            sums = sums + dot(only(v_block, h), weights, ((0,), (0,)))
+        return sums
 
     zero = jnp.zeros((blk, all_rows), jnp.float32)
-    sums = lax.fori_loop(0, n, attend_step, (zero,) * heads)
-    attended = sums[0] * inverse[0]
-    for h in range(1, heads):
-        attended = attended + sums[h] * inverse[h]
+    attended = lax.fori_loop(0, n, attend_step, zero)
     every_row = lax.broadcasted_iota(jnp.int32, (1, all_rows), 1)
     attended = jnp.where(every_row < live_count, attended, 0.0)
     attended_rows = attended.T.astype(jnp.bfloat16)
@@ -203,41 +244,31 @@
     own_att = local(att.at[rows_of(me, rows)], att_in.at[:, cols(me)], 6)
     att_moves = [send(5, d, att.at[rows_of(peer(d), rows)], att_in.at[:, cols(me)]) for d in far]
 
-    own_u.wait()
-    for copy in u_moves:
-        copy.wait_recv()
-    product = u_all[...].astype(jnp.float32) * attended_rows.astype(jnp.float32)
+    product = u_rows.astype(jnp.float32) * attended_rows.astype(jnp.float32)
     product = product.T
     delta = [jnp.sum(product[h * HD : (h + 1) * HD], axis=0, keepdims=True) for h in range(heads)]
 
     grad_q = zero
     gk_moves = []
-    gv_moves = []
-    for d in far[::-1] + [0]:
+    for d in far + [0]:
         j = peer(d)
         at = rows_of(j, tiles)
         v_block = v_all[at, :]
         k_block = k_all[at, :]
-        grad_k = grad_v = None
+        grad_k = None
         for h in range(heads):
-            query = only(q_all[...], h)
-            up = only(u_all[...], h)
-            grad_prob = dot(v_block, up, ((1,), (1,)))
-            weights = probs[h, at, :] * inverse[h]
+            query = only(q_rows, h)
+            grad_prob = dot(v_block, only(u_rows, h), ((1,), (1,)))
+            weights = probs[h, at, :]
             grad_score = (weights * (grad_prob - delta[h]) * factor).astype(jnp.bfloat16)
-            more_v = dot(weights.astype(jnp.bfloat16), up, ((1,), (0,)))
             more_k = dot(grad_score, query, ((1,), (0,)))
-            grad_v = more_v if grad_v is None else grad_v + more_v
             grad_k = more_k if grad_k is None else grad_k + more_k
             grad_q = grad_q + dot(only(k_block, h), grad_score, ((0,), (0,)))
         gk[at, :] = grad_k.astype(jnp.bfloat16)
-        gv[at, :] = grad_v.astype(jnp.bfloat16)
         if d:
             gk_moves.append(send(6, d, gk.at[at], grad_keys.at[0, :, cols(me)]))
-            gv_moves.append(send(7, d, gv.at[at], grad_values.at[0, :, cols(me)]))
         else:
             own_gk = local(gk.at[at], grad_keys.at[0, :, cols(me)], 7)
-            own_gv = local(gv.at[at], grad_values.at[0, :, cols(me)], 8)
 
     grad_rows = grad_q.T
     gq[...] = grad_rows.astype(jnp.bfloat16)
@@ -281,18 +312,31 @@
     gl_moves = [send(8, d, gq_sum.at[rows_of(peer(d), rows)], gl_in.at[:, cols(me)]) for d in far]
 
     head_move.wait_recv()
-    pooled[0] = (own_part + part_in[...].astype(jnp.float32)).astype(jnp.bfloat16)
-
+    pooled_buf[...] = (own_part + part_in[...].astype(jnp.float32)).astype(jnp.bfloat16)
+
+    out_pooled = local(pooled_buf, pooled.at[0], 10)
     own_gl.wait()
     for copy in gl_moves:
         copy.wait_recv()
-    grad_latents[...] = gl_in[...].astype(jnp.float32)
+    gl_buf[...] = gl_in[...].astype(jnp.float32)
+    out_gl = local(gl_buf, grad_latents, 11)
     own_gk.wait()
     own_gv.wait()
     for copy in gk_moves + gv_moves:
         copy.wait_recv()
-    for copy in sent + slide_moves + [head_move]:
+    for copy in sent + slide_moves + share_moves + [head_move]:
         copy.wait_send()
+    out_pooled.wait()
+    out_gl.wait()
+
+
+def finish_kernel(count, *refs):
+    sems = refs[-1]
+    copies = [pltpu.make_async_copy(refs[i], refs[count + i], sems.at[i]) for i in range(count)]
+    for copy in copies:
+        copy.start()
+    for copy in copies:
+        copy.wait()
 
 
 def swapped_body(latents, tile_keys, tile_values, tile_mask, latent_counts, out_weight, cotangent):
@@ -305,12 +349,11 @@
     heads = blk // HD
     half = depth // 2
     bf16 = jnp.bfloat16
-    anywhere = pl.BlockSpec(memory_space=pl.ANY)
+    anywhere = pl.BlockSpec(memory_space=pltpu.HBM)
     scalars = pl.BlockSpec(memory_space=pltpu.SMEM)
-    vmem = pl.BlockSpec(memory_space=pltpu.VMEM)
     dma = pltpu.SemaphoreType.DMA
     flops = 2 * heads * 6 * n * rows * n * tiles * HD + 4 * rows * width * depth
-    return pl.pallas_call(
+    results = pl.pallas_call(
         functools.partial(swap_kernel, n, slides),
         out_shape=(
             jax.ShapeDtypeStruct((1, rows, half), bf16),
@@ -319,9 +362,9 @@
             jax.ShapeDtypeStruct(tile_values.shape, bf16),
         ),
         in_specs=[anywhere, anywhere, anywhere, scalars, scalars, anywhere, anywhere],
-        out_specs=(vmem, vmem, anywhere, anywhere),
+        out_specs=(anywhere,) * 4,
         scratch_shapes=[
-            pltpu.VMEM((n * rows, blk), bf16),
+            pltpu.VMEM((n, slides, rows // slides, blk), bf16),
             pltpu.VMEM((n * tiles, blk), bf16),
             pltpu.VMEM((n * tiles, blk), bf16),
             pltpu.VMEM((n * rows, blk), bf16),
@@ -341,21 +384,33 @@
             pltpu.VMEM((slides - 1, n * rows, blk), bf16),
             pltpu.VMEM((n * rows, blk), bf16),
             pltpu.VMEM((rows, width), bf16),
-            dma((10,)),
+            pltpu.VMEM((rows, half), bf16),
+            pltpu.VMEM((rows, width), jnp.float32),
+            dma((12,)),
             dma((9, n - 1)),
             dma((9, n - 1)),
+            dma((slides - 1,)),
+            dma((slides - 1,)),
             dma((slides - 1,)),
             dma((slides - 1,)),
             dma,
             dma,
         ],
         compiler_params=pltpu.CompilerParams(
-            collective_id=0, has_side_effects=True, vmem_limit_bytes=40 * 1024 * 1024
+            collective_id=0, has_side_effects=True, vmem_limit_bytes=60 * 1024 * 1024
         ),
         cost_estimate=pl.CostEstimate(
             flops=flops, bytes_accessed=8 * rows * depth * 2, transcendentals=heads * n * rows * n * tiles
         ),
     )(latents, tile_keys, tile_values, tile_mask, latent_counts, out_weight, cotangent)
+    return pl.pallas_call(
+        functools.partial(finish_kernel, len(results)),
+        out_shape=tuple(jax.ShapeDtypeStruct(x.shape, x.dtype) for x in results),
+        in_specs=[anywhere] * len(results),
+        out_specs=(anywhere,) * len(results),
+        scratch_shapes=[dma((len(results),))],
+        compiler_params=pltpu.CompilerParams(vmem_limit_bytes=60 * 1024 * 1024),
+    )(*results)
 
 
 def body(latents, tile_keys, tile_values, tile_mask, latent_counts, out_weight, cotangent):
@@ -489,11 +544,12 @@
         P(("groups", "slide"), "seq", None),
     )
     block_width = 128 * mesh.shape["seq"]
-    swapped = mesh.shape["seq"] > 1 and mesh.shape["slide"] > 1 and mesh.shape["head"] == 2
+    swapped = mesh.shape["seq"] in (2, 4, 8) and mesh.shape["slide"] > 1 and mesh.shape["head"] == 2
 
     def chosen(latents, *others):
         by_heads = swapped and latents.shape[1] % block_width == 0
-        by_heads = by_heads and latents.shape[0] % 128 == 0 and others[0].shape[1] % BLOCK == 0
+        by_heads = by_heads and latents.shape[0] % 128 == 0
+        by_heads = by_heads and latents.shape[0] % (16 * mesh.shape["slide"]) == 0 and others[0].shape[1] % BLOCK == 0
         return (swapped_body if by_heads else body)(latents, *others)
 
     return jax.shard_map(

time: 50.9 us -> 72.6 us (1.43)
  Pallas kernels: 41.6 us -> 71.2 us
  local copies, waits for them, and re-layouts: 7.74 us -> 0 us
    pallas_call x0 -> x1, Pallas kernels: none -> 28.9 us  [swapped_body(): pl.pallas_call(functools.partial(finish_kernel, len(results)), out_shape=...]
    unnamed x16 -> x0, local copies, waits for them, and re-layouts: 7.74 us -> none
where the time goes in v2:
time: 72.6 us; the launch traced here: 72.5 us
  Pallas kernels  71.2 us (98%)
  between operations  1.29 us (2%)
    pallas_call x1, Pallas kernels, swapped_body(): pl.pallas_call(functools.partial(swap_kernel, n, slides), out_shape=(jax....  42.2 us
    pallas_call x1, Pallas kernels, swapped_body(): pl.pallas_call(functools.partial(finish_kernel, len(results)), out_shape=...  28.9 us

profile of v2, /device:TPU:0, one launch (start us, length us, event | category | flops | bytes accessed | tf_op | source)
XLA Modules:
  0.0 72.5 jit_solution(2471159926404274174)
XLA Ops:
  1.3 42.2 %shard_map.102 = (bf16[1,128,512]{2,1,0:T(8,128)(2,1)}, f32[128,512]{1,0:T(8,128)}, bf16[1,256,512]{2,1,0:T(8,128)(2,1)}, bf16[1,256,512]{2,1,0:T(8,128)(2,1)}) custom-call(bf16[128,512]{1,0:T(8,128)(2,1)} %latents.1, bf16[1,256,512]{2,1,0:T(8,128)(2,1)} %keys.1, bf16[1,256,512]{2,1,0:T(8,128)(2,1)} %values.1, s32[1,2]{1,0:T(1,128)} %mask.1, ...), custom_call_target="tpu_custom_call" | custom-call | flops 1073741824 | bytes 2097152 | tf_op jit(solution)/shard_map/pallas_call | solution.py:356
  43.5 28.9 %shard_map.103 = (bf16[1,128,512]{2,1,0:T(8,128)(2,1)}, f32[128,512]{1,0:T(8,128)}, bf16[1,256,512]{2,1,0:T(8,128)(2,1)}, bf16[1,256,512]{2,1,0:T(8,128)(2,1)}) custom-call(bf16[1,128,512]{2,1,0:T(8,128)(2,1)} %get-tuple-element.8.refs_0_, f32[128,512]{1,0:T(8,128)} %get-tuple-element.9.refs_1_, bf16[1,256,512]{2,1,0:T(8,128)(2,1)} %get-tuple-element.10.refs_2_, ...), custom_call_target="tpu_custom_call" | custom-call | tf_op jit(solution)/shard_map/pallas_call | solution.py:406

commit v3 on v2

--- a/solution.py
+++ b/solution.py
@@ -24,9 +24,9 @@
 def swap_kernel(
     n,
     slides,
-    latents,
-    keys,
-    values,
+    latents_in,
+    keys_in,
+    values_in,
     mask,
     count,
     weight,
@@ -55,8 +55,9 @@
     gq_in,
     gq_sum,
     gl_in,
-    pooled_buf,
-    gl_buf,
+    latents,
+    keys,
+    values,
     local_sem,
     send_sem,
     recv_sem,
@@ -107,12 +108,12 @@
         copy.start()
         return copy
 
+    latents_copy = local(latents_in, latents, 12)
+    keys_copy = local(keys_in, keys, 13)
+    cot_copy = local(cot.at[0], cot_buf, 1)
     w_copy = local(weight, w_buf, 0)
-    cot_copy = local(cot.at[0], cot_buf, 1)
+    values_copy = local(values_in, values, 14)
     my_share = pl.ds(pl.multiple_of(my_slide * share, 16), share)
-    own_q = local(latents.at[my_share, cols(me)], q_all.at[me, my_slide], 2)
-    own_k = local(keys.at[0, :, cols(me)], k_all.at[rows_of(me, tiles)], 3)
-    own_v = local(values.at[0, :, cols(me)], v_all.at[rows_of(me, tiles)], 4)
     mask_own[...] = jnp.zeros_like(mask_own)
     for b in range(blocks):
         mask_own[pl.ds(b, 1), :] = jnp.full((1, 128), mask[0, b], jnp.int32)
@@ -136,7 +137,11 @@
     far = [n // 2] + [d for d in range(n - 1, 0, -1) if d != n // 2]
     pl.semaphore_wait(barrier, n - 1 + slides - 1 + 1)
     mask_moves = [send(0, d, mask_own, mask_all.at[me]) for d in far]
+    latents_copy.wait()
+    own_q = local(latents.at[my_share, cols(me)], q_all.at[me, my_slide], 2)
     q_moves = [send(1, d, latents.at[my_share, cols(peer(d))], q_all.at[me, my_slide]) for d in far]
+    keys_copy.wait()
+    own_k = local(keys.at[0, :, cols(me)], k_all.at[rows_of(me, tiles)], 3)
     k_moves = [send(2, d, keys.at[0, :, cols(peer(d))], k_all.at[rows_of(me, tiles)]) for d in far]
 
     live_count = count[0]
@@ -148,6 +153,8 @@
     own_u = local(u_own.at[:, cols(me)], u_all.at[rows_of(me, rows)], 5)
     u_moves = [send(4, d, u_own.at[:, cols(peer(d))], u_all.at[rows_of(me, rows)]) for d in far]
 
+    values_copy.wait()
+    own_v = local(values.at[0, :, cols(me)], v_all.at[rows_of(me, tiles)], 4)
     v_moves = [send(3, d, values.at[0, :, cols(peer(d))], v_all.at[rows_of(me, tiles)]) for d in far]
 
     lane = lax.broadcasted_iota(jnp.int32, (1, blk), 1) // HD
@@ -312,22 +319,18 @@
     gl_moves = [send(8, d, gq_sum.at[rows_of(peer(d), rows)], gl_in.at[:, cols(me)]) for d in far]
 
     head_move.wait_recv()
-    pooled_buf[...] = (own_part + part_in[...].astype(jnp.float32)).astype(jnp.bfloat16)
-
-    out_pooled = local(pooled_buf, pooled.at[0], 10)
+    pooled[0] = (own_part + part_in[...].astype(jnp.float32)).astype(jnp.bfloat16)
+
     own_gl.wait()
     for copy in gl_moves:
         copy.wait_recv()
-    gl_buf[...] = gl_in[...].astype(jnp.float32)
-    out_gl = local(gl_buf, grad_latents, 11)
+    grad_latents[...] = gl_in[...].astype(jnp.float32)
     own_gk.wait()
     own_gv.wait()
     for copy in gk_moves + gv_moves:
         copy.wait_recv()
     for copy in sent + slide_moves + share_moves + [head_move]:
         copy.wait_send()
-    out_pooled.wait()
-    out_gl.wait()
 
 
 def finish_kernel(count, *refs):
@@ -349,20 +352,20 @@
     heads = blk // HD
     half = depth // 2
     bf16 = jnp.bfloat16
-    anywhere = pl.BlockSpec(memory_space=pltpu.HBM)
+    anywhere = pl.BlockSpec(memory_space=pl.ANY)
     scalars = pl.BlockSpec(memory_space=pltpu.SMEM)
     dma = pltpu.SemaphoreType.DMA
     flops = 2 * heads * 6 * n * rows * n * tiles * HD + 4 * rows * width * depth
     results = pl.pallas_call(
         functools.partial(swap_kernel, n, slides),
         out_shape=(
-            jax.ShapeDtypeStruct((1, rows, half), bf16),
-            jax.ShapeDtypeStruct((rows, width), jnp.float32),
-            jax.ShapeDtypeStruct(tile_keys.shape, bf16),
-            jax.ShapeDtypeStruct(tile_values.shape, bf16),
+            pltpu.VMEM((1, rows, half), bf16),
+            pltpu.VMEM((rows, width), jnp.float32),
+            pltpu.VMEM(tile_keys.shape, bf16),
+            pltpu.VMEM(tile_values.shape, bf16),
         ),
         in_specs=[anywhere, anywhere, anywhere, scalars, scalars, anywhere, anywhere],
-        out_specs=(anywhere,) * 4,
+        out_specs=(pl.BlockSpec(memory_space=pltpu.VMEM),) * 4,
         scratch_shapes=[
             pltpu.VMEM((n, slides, rows // slides, blk), bf16),
             pltpu.VMEM((n * tiles, blk), bf16),
@@ -384,9 +387,10 @@
             pltpu.VMEM((slides - 1, n * rows, blk), bf16),
             pltpu.VMEM((n * rows, blk), bf16),
             pltpu.VMEM((rows, width), bf16),
-            pltpu.VMEM((rows, half), bf16),
-            pltpu.VMEM((rows, width), jnp.float32),
-            dma((12,)),
+            pltpu.VMEM(latents.shape, bf16),
+            pltpu.VMEM(tile_keys.shape, bf16),
+            pltpu.VMEM(tile_values.shape, bf16),
+            dma((15,)),
             dma((9, n - 1)),
             dma((9, n - 1)),
             dma((slides - 1,)),
@@ -409,7 +413,7 @@
         in_specs=[anywhere] * len(results),
         out_specs=(anywhere,) * len(results),
         scratch_shapes=[dma((len(results),))],
-        compiler_params=pltpu.CompilerParams(vmem_limit_bytes=60 * 1024 * 1024),
+        compiler_params=pltpu.CompilerParams(vmem_limit_bytes=4 * 1024 * 1024),
     )(*results)
 
 

time: 72.6 us -> 44.1 us (0.61)
  Pallas kernels: 71.2 us -> 42.7 us
    pallas_call x1, Pallas kernels: 28.9 us -> 0.96 us  [swapped_body(): pl.pallas_call(functools.partial(finish_kernel, len(results)), out_shape=...]
where the time goes in v3:
time: 44.1 us; the launch traced here: 44 us
  Pallas kernels  42.7 us (97%)
  between operations  1.29 us (3%)
    pallas_call x1, Pallas kernels, swapped_body(): pl.pallas_call(functools.partial(swap_kernel, n, slides), out_shape=(pltp...  41.7 us
    pallas_call x1, Pallas kernels, swapped_body(): pl.pallas_call(functools.partial(finish_kernel, len(results)), out_shape=...  0.96 us

profile of v3, /device:TPU:0, one launch (start us, length us, event | category | flops | bytes accessed | tf_op | source)
XLA Modules:
  0.0 44.0 jit_solution(9942045445061491229)
XLA Ops:
  1.3 41.7 %shard_map.102 = (bf16[1,128,512]{2,1,0:T(8,128)(2,1)S(1)}, f32[128,512]{1,0:T(8,128)S(1)}, bf16[1,256,512]{2,1,0:T(8,128)(2,1)S(1)}, bf16[1,256,512]{2,1,0:T(8,128)(2,1)S(1)}) custom-call(bf16[128,512]{1,0:T(8,128)(2,1)} %latents_in.1, bf16[1,256,512]{2,1,0:T(8,128)(2,1)} %keys_in.1, bf16[1,256,512]{2,1,0:T(8,128)(2,1)} %values_in.1, s32[1,2]{1,0:T(1,128)} %mask.1, ...), custom_call_target="tpu_custom_call" | custom-call | flops 1073741824 | bytes 2097152 | tf_op jit(solution)/shard_map/pallas_call | solution.py:359
  43.0 1.0 %shard_map.103 = (bf16[1,128,512]{2,1,0:T(8,128)(2,1)}, f32[128,512]{1,0:T(8,128)}, bf16[1,256,512]{2,1,0:T(8,128)(2,1)}, bf16[1,256,512]{2,1,0:T(8,128)(2,1)}) custom-call(bf16[1,128,512]{2,1,0:T(8,128)(2,1)S(1)} %get-tuple-element.8.refs_0_, f32[128,512]{1,0:T(8,128)S(1)} %get-tuple-element.9.refs_1_, bf16[1,256,512]{2,1,0:T(8,128)(2,1)S(1)} %get-tuple-element.10.refs_2_, ...), custom_call_target="tpu_custom_call" | custom-call | tf_op jit(solution)/shard_map/pallas_call | solution.py:410

commit v4 on v3

--- a/solution.py
+++ b/solution.py
@@ -153,10 +153,6 @@
     own_u = local(u_own.at[:, cols(me)], u_all.at[rows_of(me, rows)], 5)
     u_moves = [send(4, d, u_own.at[:, cols(peer(d))], u_all.at[rows_of(me, rows)]) for d in far]
 
-    values_copy.wait()
-    own_v = local(values.at[0, :, cols(me)], v_all.at[rows_of(me, tiles)], 4)
-    v_moves = [send(3, d, values.at[0, :, cols(peer(d))], v_all.at[rows_of(me, tiles)]) for d in far]
-
     lane = lax.broadcasted_iota(jnp.int32, (1, blk), 1) // HD
 
     def only(x, h):
@@ -180,6 +176,10 @@
     own_k.wait()
     for copy in mask_moves + share_moves + k_moves:
         copy.wait_recv()
+    values_copy.wait()
+    own_v = local(values.at[0, :, cols(me)], v_all.at[rows_of(me, tiles)], 4)
+    v_moves = [send(3, d, values.at[0, :, cols(peer(d))], v_all.at[rows_of(me, tiles)]) for d in far]
+
     q_rows = q_all[...].reshape(all_rows, blk)
 
     tops = []
@@ -188,9 +188,10 @@
         query = only(q_rows, h)
 
         def score_step(i, top, h=h, query=query):
+            scores = dot(k_all[rows_of(i, tiles), :], query, ((1,), (1,))) * factor
             for b in range(blocks):
                 at = pl.ds(pl.multiple_of(i * tiles + b * BLOCK, BLOCK), BLOCK)
-                score = dot(k_all[at, :], query, ((1,), (1,))) * factor
+                score = scores[b * BLOCK : (b + 1) * BLOCK]
                 valid = jnp.broadcast_to(mask_all[i][b : b + 1, :1], (1, all_rows)) > 0
                 score = jnp.where(valid, score, masked_score)
                 probs[h, at, :] = score

time: 44.1 us -> 44.1 us (level)
  no operation moved by 1% of the time
where the time goes in v4:
time: 44.1 us; the launch traced here: 44 us
  Pallas kernels  42.7 us (97%)
  between operations  1.29 us (3%)
    pallas_call x1, Pallas kernels, swapped_body(): pl.pallas_call(functools.partial(swap_kernel, n, slides), out_shape=(pltp...  41.7 us
    pallas_call x1, Pallas kernels, swapped_body(): pl.pallas_call(functools.partial(finish_kernel, len(results)), out_shape=...  0.96 us

profile of v4, /device:TPU:0, one launch (start us, length us, event | category | flops | bytes accessed | tf_op | source)
XLA Modules:
  0.0 44.0 jit_solution(6976974342092773549)
XLA Ops:
  1.3 41.7 %shard_map.102 = (bf16[1,128,512]{2,1,0:T(8,128)(2,1)S(1)}, f32[128,512]{1,0:T(8,128)S(1)}, bf16[1,256,512]{2,1,0:T(8,128)(2,1)S(1)}, bf16[1,256,512]{2,1,0:T(8,128)(2,1)S(1)}) custom-call(bf16[128,512]{1,0:T(8,128)(2,1)} %latents_in.1, bf16[1,256,512]{2,1,0:T(8,128)(2,1)} %keys_in.1, bf16[1,256,512]{2,1,0:T(8,128)(2,1)} %values_in.1, s32[1,2]{1,0:T(1,128)} %mask.1, ...), custom_call_target="tpu_custom_call" | custom-call | flops 1073741824 | bytes 2097152 | tf_op jit(solution)/shard_map/pallas_call | solution.py:360
  43.0 1.0 %shard_map.103 = (bf16[1,128,512]{2,1,0:T(8,128)(2,1)}, f32[128,512]{1,0:T(8,128)}, bf16[1,256,512]{2,1,0:T(8,128)(2,1)}, bf16[1,256,512]{2,1,0:T(8,128)(2,1)}) custom-call(bf16[1,128,512]{2,1,0:T(8,128)(2,1)S(1)} %get-tuple-element.8.refs_0_, f32[128,512]{1,0:T(8,128)S(1)} %get-tuple-element.9.refs_1_, bf16[1,256,512]{2,1,0:T(8,128)(2,1)S(1)} %get-tuple-element.10.refs_2_, ...), custom_call_target="tpu_custom_call" | custom-call | tf_op jit(solution)/shard_map/pallas_call | solution.py:411

commit v5 on v4

--- a/solution.py
+++ b/solution.py
@@ -15,6 +15,7 @@
 
 
 MESH = pl.DeviceIdType.MESH
+PAIR = 2
 
 
 def dot(a, b, dims):
@@ -58,6 +59,10 @@
     latents,
     keys,
     values,
+    stats,
+    stats_in,
+    deltas,
+    deltas_in,
     local_sem,
     send_sem,
     recv_sem,
@@ -69,6 +74,9 @@
     head_recv,
 ):
     me = lax.axis_index("seq")
+    g = PAIR
+    side = lax.rem(me, g)
+    part = lax.div(me, g)
     my_head = lax.axis_index("head")
     my_slide = lax.axis_index("slide")
     rows = latents.shape[0]
@@ -87,6 +95,9 @@
     def rows_of(j, size):
         return pl.ds(pl.multiple_of(j * size, 128), size)
 
+    def cols_for(d):
+        return cols(lax.rem(peer(d), g))
+
     def peer(d):
         other, bit = me, 1
         while bit < n:
@@ -117,7 +128,7 @@
     mask_own[...] = jnp.zeros_like(mask_own)
     for b in range(blocks):
         mask_own[pl.ds(b, 1), :] = jnp.full((1, 128), mask[0, b], jnp.int32)
-    mask_all[me] = mask_own[...]
+    mask_all[side] = mask_own[...]
 
     sent = []
 
@@ -136,13 +147,13 @@
 
     far = [n // 2] + [d for d in range(n - 1, 0, -1) if d != n // 2]
     pl.semaphore_wait(barrier, n - 1 + slides - 1 + 1)
-    mask_moves = [send(0, d, mask_own, mask_all.at[me]) for d in far]
+    mask_moves = [send(0, 1, mask_own, mask_all.at[side])]
     latents_copy.wait()
-    own_q = local(latents.at[my_share, cols(me)], q_all.at[me, my_slide], 2)
-    q_moves = [send(1, d, latents.at[my_share, cols(peer(d))], q_all.at[me, my_slide]) for d in far]
+    own_q = local(latents.at[my_share, cols(side)], q_all.at[me, my_slide], 2)
+    q_moves = [send(1, d, latents.at[my_share, cols_for(d)], q_all.at[me, my_slide]) for d in far]
     keys_copy.wait()
-    own_k = local(keys.at[0, :, cols(me)], k_all.at[rows_of(me, tiles)], 3)
-    k_moves = [send(2, d, keys.at[0, :, cols(peer(d))], k_all.at[rows_of(me, tiles)]) for d in far]
+    own_k = local(keys.at[0, :, cols(side)], k_all.at[rows_of(side, tiles)], 3)
+    k_moves = [send(2, 1, keys.at[0, :, cols_for(1)], k_all.at[rows_of(side, tiles)])]
 
     live_count = count[0]
     w_copy.wait()
@@ -150,8 +161,8 @@
     own_row = lax.broadcasted_iota(jnp.int32, (rows, 1), 0) + me * rows
     projected = dot(cot_buf[...], w_buf[...], ((1,), (1,)))
     u_own[...] = jnp.where(own_row < live_count, projected, 0.0).astype(jnp.bfloat16)
-    own_u = local(u_own.at[:, cols(me)], u_all.at[rows_of(me, rows)], 5)
-    u_moves = [send(4, d, u_own.at[:, cols(peer(d))], u_all.at[rows_of(me, rows)]) for d in far]
+    own_u = local(u_own.at[:, cols(side)], u_all.at[rows_of(me, rows)], 5)
+    u_moves = [send(4, d, u_own.at[:, cols_for(d)], u_all.at[rows_of(me, rows)]) for d in far]
 
     lane = lax.broadcasted_iota(jnp.int32, (1, blk), 1) // HD
 
@@ -177,8 +188,8 @@
     for copy in mask_moves + share_moves + k_moves:
         copy.wait_recv()
     values_copy.wait()
-    own_v = local(values.at[0, :, cols(me)], v_all.at[rows_of(me, tiles)], 4)
-    v_moves = [send(3, d, values.at[0, :, cols(peer(d))], v_all.at[rows_of(me, tiles)]) for d in far]
+    own_v = local(values.at[0, :, cols(side)], v_all.at[rows_of(side, tiles)], 4)
+    v_moves = [send(3, 1, values.at[0, :, cols_for(1)], v_all.at[rows_of(side, tiles)])]
 
     q_rows = q_all[...].reshape(all_rows, blk)
 
@@ -198,7 +209,9 @@
                 top = jnp.maximum(top, jnp.max(score, axis=0, keepdims=True))
             return top
 
-        top = lax.fori_loop(0, n, score_step, jnp.full((1, all_rows), masked_score, jnp.float32))
+        top = lax.fori_loop(0, g, score_step, jnp.full((1, all_rows), masked_score, jnp.float32))
+
+        tops.append(top)
 
         def exp_step(i, total, h=h, top=top):
             for b in range(blocks):
@@ -208,17 +221,31 @@
                 total = total + jnp.sum(expos, axis=0, keepdims=True)
             return total
 
-        totals.append(lax.fori_loop(0, n, exp_step, jnp.zeros((1, all_rows), jnp.float32)))
-    inverse = [1.0 / total for total in totals]
+        totals.append(lax.fori_loop(0, g, exp_step, jnp.zeros((1, all_rows), jnp.float32)))
+    stats[...] = jnp.zeros_like(stats)
+    for h in range(heads):
+        stats[pl.ds(h, 1), :] = tops[h]
+        stats[pl.ds(heads + h, 1), :] = totals[h]
+    stat_moves = [send(9, d, stats, stats_in.at[d // g - 1]) for d in range(g, n, g)]
+    for copy in stat_moves:
+        copy.wait_recv()
+    inverse = []
+    for h in range(heads):
+        other_tops = [stats_in[e, h : h + 1, :] for e in range(n // g - 1)]
+        whole_top = functools.reduce(jnp.maximum, other_tops, tops[h])
+        whole_total = totals[h] * jnp.exp(tops[h] - whole_top)
+        for e, other in enumerate(other_tops):
+            more = stats_in[e, heads + h : heads + h + 1, :]
+            whole_total = whole_total + more * jnp.exp(other - whole_top)
+        inverse.append(jnp.exp(tops[h] - whole_top) / whole_total)
 
     own_u.wait()
     for copy in u_moves:
         copy.wait_recv()
     u_rows = u_all[...]
     gv_moves = []
-    for d in far + [0]:
-        j = peer(d)
-        at = rows_of(j, tiles)
+    for d in (1, 0):
+        at = rows_of(lax.rem(peer(d), g), tiles)
         grad_v = None
         for h in range(heads):
             weights = probs[h, at, :] * inverse[h]
@@ -227,9 +254,9 @@
             grad_v = more_v if grad_v is None else grad_v + more_v
         gv[at, :] = grad_v.astype(jnp.bfloat16)
         if d:
-            gv_moves.append(send(7, d, gv.at[at], grad_values.at[0, :, cols(me)]))
+            gv_moves.append(send(7, d, gv.at[at], grad_values.at[0, :, cols(side)]))
         else:
-            own_gv = local(gv.at[at], grad_values.at[0, :, cols(me)], 8)
+            own_gv = local(gv.at[at], grad_values.at[0, :, cols(side)], 8)
 
     own_v.wait()
     for copy in v_moves:
@@ -244,23 +271,28 @@
         return sums
 
     zero = jnp.zeros((blk, all_rows), jnp.float32)
-    attended = lax.fori_loop(0, n, attend_step, zero)
+    attended = lax.fori_loop(0, g, attend_step, zero)
     every_row = lax.broadcasted_iota(jnp.int32, (1, all_rows), 1)
     attended = jnp.where(every_row < live_count, attended, 0.0)
     attended_rows = attended.T.astype(jnp.bfloat16)
     att[...] = attended_rows
-    own_att = local(att.at[rows_of(me, rows)], att_in.at[:, cols(me)], 6)
-    att_moves = [send(5, d, att.at[rows_of(peer(d), rows)], att_in.at[:, cols(me)]) for d in far]
-
-    product = u_rows.astype(jnp.float32) * attended_rows.astype(jnp.float32)
-    product = product.T
+    own_att = local(att.at[rows_of(me, rows)], att_in.at[part, :, cols(side)], 6)
+    att_moves = [send(5, d, att.at[rows_of(peer(d), rows)], att_in.at[part, :, cols(side)]) for d in far]
+
+    product = u_rows.astype(jnp.float32).T * attended
     delta = [jnp.sum(product[h * HD : (h + 1) * HD], axis=0, keepdims=True) for h in range(heads)]
+    deltas[...] = jnp.zeros_like(deltas)
+    for h in range(heads):
+        deltas[pl.ds(h, 1), :] = delta[h]
+    delta_moves = [send(10, d, deltas, deltas_in.at[d // g - 1]) for d in range(g, n, g)]
+    for e, copy in enumerate(delta_moves):
+        copy.wait_recv()
+        delta = [delta[h] + deltas_in[e, h : h + 1, :] for h in range(heads)]
 
     grad_q = zero
     gk_moves = []
-    for d in far + [0]:
-        j = peer(d)
-        at = rows_of(j, tiles)
+    for d in (1, 0):
+        at = rows_of(lax.rem(peer(d), g), tiles)
         v_block = v_all[at, :]
         k_block = k_all[at, :]
         grad_k = None
@@ -274,9 +306,9 @@
             grad_q = grad_q + dot(only(k_block, h), grad_score, ((0,), (0,)))
         gk[at, :] = grad_k.astype(jnp.bfloat16)
         if d:
-            gk_moves.append(send(6, d, gk.at[at], grad_keys.at[0, :, cols(me)]))
+            gk_moves.append(send(6, d, gk.at[at], grad_keys.at[0, :, cols(side)]))
         else:
-            own_gk = local(gk.at[at], grad_keys.at[0, :, cols(me)], 7)
+            own_gk = local(gk.at[at], grad_keys.at[0, :, cols(side)], 7)
 
     grad_rows = grad_q.T
     gq[...] = grad_rows.astype(jnp.bfloat16)
@@ -299,7 +331,11 @@
     half = pooled.shape[2]
     mine = pl.ds(pl.multiple_of(my_head * half, 128), half)
     theirs = pl.ds(pl.multiple_of((1 - my_head) * half, 128), half)
-    part_out[...] = dot(att_in[...], w_buf[:, theirs], ((1,), (0,))).astype(jnp.bfloat16)
+    att_sum = att_in[0].astype(jnp.float32)
+    for e in range(1, n // g):
+        att_sum = att_sum + att_in[e].astype(jnp.float32)
+    att_sum = att_sum.astype(jnp.bfloat16)
+    part_out[...] = dot(att_sum, w_buf[:, theirs], ((1,), (0,))).astype(jnp.bfloat16)
     head_move = pltpu.make_async_remote_copy(
         src_ref=part_out,
         dst_ref=part_in,
@@ -309,15 +345,15 @@
         device_id_type=MESH,
     )
     head_move.start()
-    own_part = dot(att_in[...], w_buf[:, mine], ((1,), (0,)))
+    own_part = dot(att_sum, w_buf[:, mine], ((1,), (0,)))
 
     total = grad_rows
     for e, copy in enumerate(slide_moves):
         copy.wait_recv()
         total = total + gq_in[e].astype(jnp.float32)
     gq_sum[...] = total.astype(jnp.bfloat16)
-    own_gl = local(gq_sum.at[rows_of(me, rows)], gl_in.at[:, cols(me)], 9)
-    gl_moves = [send(8, d, gq_sum.at[rows_of(peer(d), rows)], gl_in.at[:, cols(me)]) for d in far]
+    own_gl = local(gq_sum.at[rows_of(me, rows)], gl_in.at[part, :, cols(side)], 9)
+    gl_moves = [send(8, d, gq_sum.at[rows_of(peer(d), rows)], gl_in.at[part, :, cols(side)]) for d in far]
 
     head_move.wait_recv()
     pooled[0] = (own_part + part_in[...].astype(jnp.float32)).astype(jnp.bfloat16)
@@ -325,7 +361,10 @@
     own_gl.wait()
     for copy in gl_moves:
         copy.wait_recv()
-    grad_latents[...] = gl_in[...].astype(jnp.float32)
+    gl_sum = gl_in[0].astype(jnp.float32)
+    for e in range(1, n // g):
+        gl_sum = gl_sum + gl_in[e].astype(jnp.float32)
+    grad_latents[...] = gl_sum
     own_gk.wait()
     own_gv.wait()
     for copy in gk_moves + gv_moves:
@@ -349,14 +388,15 @@
     rows, width = latents.shape
     tiles = tile_keys.shape[1]
     depth = out_weight.shape[1]
-    blk = width // n
+    g = PAIR
+    blk = width // g
     heads = blk // HD
     half = depth // 2
     bf16 = jnp.bfloat16
     anywhere = pl.BlockSpec(memory_space=pl.ANY)
     scalars = pl.BlockSpec(memory_space=pltpu.SMEM)
     dma = pltpu.SemaphoreType.DMA
-    flops = 2 * heads * 6 * n * rows * n * tiles * HD + 4 * rows * width * depth
+    flops = 2 * heads * 6 * n * rows * g * tiles * HD + 4 * rows * width * depth
     results = pl.pallas_call(
         functools.partial(swap_kernel, n, slides),
         out_shape=(
@@ -369,31 +409,35 @@
         out_specs=(pl.BlockSpec(memory_space=pltpu.VMEM),) * 4,
         scratch_shapes=[
             pltpu.VMEM((n, slides, rows // slides, blk), bf16),
-            pltpu.VMEM((n * tiles, blk), bf16),
-            pltpu.VMEM((n * tiles, blk), bf16),
+            pltpu.VMEM((g * tiles, blk), bf16),
+            pltpu.VMEM((g * tiles, blk), bf16),
             pltpu.VMEM((n * rows, blk), bf16),
             pltpu.VMEM((8 * pl.cdiv(tiles // BLOCK, 8), 128), jnp.int32),
-            pltpu.VMEM((n, 8 * pl.cdiv(tiles // BLOCK, 8), 128), jnp.int32),
+            pltpu.VMEM((g, 8 * pl.cdiv(tiles // BLOCK, 8), 128), jnp.int32),
             pltpu.VMEM((width, depth), bf16),
             pltpu.VMEM((rows, depth), bf16),
             pltpu.VMEM((rows, width), bf16),
-            pltpu.VMEM((heads, n * tiles, n * rows), jnp.float32),
+            pltpu.VMEM((heads, g * tiles, n * rows), jnp.float32),
             pltpu.VMEM((n * rows, blk), bf16),
-            pltpu.VMEM((rows, width), bf16),
+            pltpu.VMEM((n // g, rows, width), bf16),
             pltpu.VMEM((rows, half), bf16),
             pltpu.VMEM((rows, half), bf16),
-            pltpu.VMEM((n * tiles, blk), bf16),
-            pltpu.VMEM((n * tiles, blk), bf16),
+            pltpu.VMEM((g * tiles, blk), bf16),
+            pltpu.VMEM((g * tiles, blk), bf16),
             pltpu.VMEM((n * rows, blk), bf16),
             pltpu.VMEM((slides - 1, n * rows, blk), bf16),
             pltpu.VMEM((n * rows, blk), bf16),
-            pltpu.VMEM((rows, width), bf16),
+            pltpu.VMEM((n // g, rows, width), bf16),
             pltpu.VMEM(latents.shape, bf16),
             pltpu.VMEM(tile_keys.shape, bf16),
             pltpu.VMEM(tile_values.shape, bf16),
+            pltpu.VMEM((8 * pl.cdiv(2 * heads, 8), n * rows), jnp.float32),
+            pltpu.VMEM((n // g - 1, 8 * pl.cdiv(2 * heads, 8), n * rows), jnp.float32),
+            pltpu.VMEM((8 * pl.cdiv(heads, 8), n * rows), jnp.float32),
+            pltpu.VMEM((n // g - 1, 8 * pl.cdiv(heads, 8), n * rows), jnp.float32),
             dma((15,)),
-            dma((9, n - 1)),
-            dma((9, n - 1)),
+            dma((11, n - 1)),
+            dma((11, n - 1)),
             dma((slides - 1,)),
             dma((slides - 1,)),
             dma((slides - 1,)),
@@ -405,7 +449,7 @@
             collective_id=0, has_side_effects=True, vmem_limit_bytes=60 * 1024 * 1024
         ),
         cost_estimate=pl.CostEstimate(
-            flops=flops, bytes_accessed=8 * rows * depth * 2, transcendentals=heads * n * rows * n * tiles
+            flops=flops, bytes_accessed=8 * rows * depth * 2, transcendentals=heads * n * rows * g * tiles
         ),
     )(latents, tile_keys, tile_values, tile_mask, latent_counts, out_weight, cotangent)
     return pl.pallas_call(
@@ -548,8 +592,8 @@
         P("head", None),
         P(("groups", "slide"), "seq", None),
     )
-    block_width = 128 * mesh.shape["seq"]
-    swapped = mesh.shape["seq"] in (2, 4, 8) and mesh.shape["slide"] > 1 and mesh.shape["head"] == 2
+    block_width = 128 * PAIR
+    swapped = mesh.shape["seq"] in (4, 8) and mesh.shape["slide"] > 1 and mesh.shape["head"] == 2
 
     def chosen(latents, *others):
         by_heads = swapped and latents.shape[1] % block_width == 0

time: 44.1 us -> 46.4 us (1.052)
  Pallas kernels: 42.7 us -> 45 us
    pallas_call x1, Pallas kernels: 41.7 us -> 44 us  [swapped_body(): pl.pallas_call(functools.partial(swap_kernel, n, slides), out_shape=(pltp...]
where the time goes in v5:
time: 46.4 us; the launch traced here: 46.2 us
  Pallas kernels  45 us (97%)
  between operations  1.29 us (3%)
    pallas_call x1, Pallas kernels, swapped_body(): pl.pallas_call(functools.partial(swap_kernel, n, slides), out_shape=(pltp...  44 us
    pallas_call x1, Pallas kernels, swapped_body(): pl.pallas_call(functools.partial(finish_kernel, len(results)), out_shape=...  0.96 us

profile of v5, /device:TPU:0, one launch (start us, length us, event | category | flops | bytes accessed | tf_op | source)
XLA Modules:
  0.0 46.2 jit_solution(5104876808543462158)
XLA Ops:
  1.3 44.0 %shard_map.102 = (bf16[1,128,512]{2,1,0:T(8,128)(2,1)S(1)}, f32[128,512]{1,0:T(8,128)S(1)}, bf16[1,256,512]{2,1,0:T(8,128)(2,1)S(1)}, bf16[1,256,512]{2,1,0:T(8,128)(2,1)S(1)}) custom-call(bf16[128,512]{1,0:T(8,128)(2,1)} %latents_in.1, bf16[1,256,512]{2,1,0:T(8,128)(2,1)} %keys_in.1, bf16[1,256,512]{2,1,0:T(8,128)(2,1)} %values_in.1, s32[1,2]{1,0:T(1,128)} %mask.1, ...), custom_call_target="tpu_custom_call" | custom-call | flops 1073741824 | bytes 2097152 | tf_op jit(solution)/shard_map/pallas_call | solution.py:400
  45.3 1.0 %shard_map.103 = (bf16[1,128,512]{2,1,0:T(8,128)(2,1)}, f32[128,512]{1,0:T(8,128)}, bf16[1,256,512]{2,1,0:T(8,128)(2,1)}, bf16[1,256,512]{2,1,0:T(8,128)(2,1)}) custom-call(bf16[1,128,512]{2,1,0:T(8,128)(2,1)S(1)} %get-tuple-element.8.refs_0_, f32[128,512]{1,0:T(8,128)S(1)} %get-tuple-element.9.refs_1_, bf16[1,256,512]{2,1,0:T(8,128)(2,1)S(1)} %get-tuple-element.10.refs_2_, ...), custom_call_target="tpu_custom_call" | custom-call | tf_op jit(solution)/shard_map/pallas_call | solution.py:455

commit v6 on v4

--- a/solution.py
+++ b/solution.py
@@ -45,6 +45,7 @@
     cot_buf,
     u_own,
     probs,
+    grad_scores,
     att,
     att_in,
     part_out,
@@ -257,26 +258,15 @@
     delta = [jnp.sum(product[h * HD : (h + 1) * HD], axis=0, keepdims=True) for h in range(heads)]
 
     grad_q = zero
-    gk_moves = []
     for d in far + [0]:
-        j = peer(d)
-        at = rows_of(j, tiles)
+        at = rows_of(peer(d), tiles)
         v_block = v_all[at, :]
         k_block = k_all[at, :]
-        grad_k = None
         for h in range(heads):
-            query = only(q_rows, h)
             grad_prob = dot(v_block, only(u_rows, h), ((1,), (1,)))
-            weights = probs[h, at, :]
-            grad_score = (weights * (grad_prob - delta[h]) * factor).astype(jnp.bfloat16)
-            more_k = dot(grad_score, query, ((1,), (0,)))
-            grad_k = more_k if grad_k is None else grad_k + more_k
+            grad_score = (probs[h, at, :] * (grad_prob - delta[h]) * factor).astype(jnp.bfloat16)
+            grad_scores[h, at, :] = grad_score
             grad_q = grad_q + dot(only(k_block, h), grad_score, ((0,), (0,)))
-        gk[at, :] = grad_k.astype(jnp.bfloat16)
-        if d:
-            gk_moves.append(send(6, d, gk.at[at], grad_keys.at[0, :, cols(me)]))
-        else:
-            own_gk = local(gk.at[at], grad_keys.at[0, :, cols(me)], 7)
 
     grad_rows = grad_q.T
     gq[...] = grad_rows.astype(jnp.bfloat16)
@@ -293,6 +283,26 @@
         copy.start()
         slide_moves.append(copy)
 
+    gk_moves = []
+    for d in far + [0]:
+        at = rows_of(peer(d), tiles)
+        grad_k = dot(grad_scores[0, at, :], only(q_rows, 0), ((1,), (0,)))
+        for h in range(1, heads):
+            grad_k = grad_k + dot(grad_scores[h, at, :], only(q_rows, h), ((1,), (0,)))
+        gk[at, :] = grad_k.astype(jnp.bfloat16)
+        if d:
+            gk_moves.append(send(6, d, gk.at[at], grad_keys.at[0, :, cols(me)]))
+        else:
+            own_gk = local(gk.at[at], grad_keys.at[0, :, cols(me)], 7)
+
+    total = grad_rows
+    for e, copy in enumerate(slide_moves):
+        copy.wait_recv()
+        total = total + gq_in[e].astype(jnp.float32)
+    gq_sum[...] = total.astype(jnp.bfloat16)
+    own_gl = local(gq_sum.at[rows_of(me, rows)], gl_in.at[:, cols(me)], 9)
+    gl_moves = [send(8, d, gq_sum.at[rows_of(peer(d), rows)], gl_in.at[:, cols(me)]) for d in far]
+
     own_att.wait()
     for copy in att_moves:
         copy.wait_recv()
@@ -310,14 +320,6 @@
     )
     head_move.start()
     own_part = dot(att_in[...], w_buf[:, mine], ((1,), (0,)))
-
-    total = grad_rows
-    for e, copy in enumerate(slide_moves):
-        copy.wait_recv()
-        total = total + gq_in[e].astype(jnp.float32)
-    gq_sum[...] = total.astype(jnp.bfloat16)
-    own_gl = local(gq_sum.at[rows_of(me, rows)], gl_in.at[:, cols(me)], 9)
-    gl_moves = [send(8, d, gq_sum.at[rows_of(peer(d), rows)], gl_in.at[:, cols(me)]) for d in far]
 
     head_move.wait_recv()
     pooled[0] = (own_part + part_in[...].astype(jnp.float32)).astype(jnp.bfloat16)
@@ -378,6 +380,7 @@
             pltpu.VMEM((rows, depth), bf16),
             pltpu.VMEM((rows, width), bf16),
             pltpu.VMEM((heads, n * tiles, n * rows), jnp.float32),
+            pltpu.VMEM((heads, n * tiles, n * rows), bf16),
             pltpu.VMEM((n * rows, blk), bf16),
             pltpu.VMEM((rows, width), bf16),
             pltpu.VMEM((rows, half), bf16),

time: 44.1 us -> 44.2 us (level)
  no operation moved by 1% of the time
where the time goes in v6:
time: 44.2 us; the launch traced here: 44 us
  Pallas kernels  42.8 us (97%)
  between operations  1.29 us (3%)
    pallas_call x1, Pallas kernels, swapped_body(): pl.pallas_call(functools.partial(swap_kernel, n, slides), out_shape=(pltp...  41.8 us
    pallas_call x1, Pallas kernels, swapped_body(): pl.pallas_call(functools.partial(finish_kernel, len(results)), out_shape=...  0.96 us

profile of v6, /device:TPU:0, one launch (start us, length us, event | category | flops | bytes accessed | tf_op | source)
XLA Modules:
  0.0 44.0 jit_solution(2487072732624698361)
XLA Ops:
  1.3 41.8 %shard_map.102 = (bf16[1,128,512]{2,1,0:T(8,128)(2,1)S(1)}, f32[128,512]{1,0:T(8,128)S(1)}, bf16[1,256,512]{2,1,0:T(8,128)(2,1)S(1)}, bf16[1,256,512]{2,1,0:T(8,128)(2,1)S(1)}) custom-call(bf16[128,512]{1,0:T(8,128)(2,1)} %latents_in.1, bf16[1,256,512]{2,1,0:T(8,128)(2,1)} %keys_in.1, bf16[1,256,512]{2,1,0:T(8,128)(2,1)} %values_in.1, s32[1,2]{1,0:T(1,128)} %mask.1, ...), custom_call_target="tpu_custom_call" | custom-call | flops 1073741824 | bytes 2097152 | tf_op jit(solution)/shard_map/pallas_call | solution.py:362
  43.1 1.0 %shard_map.103 = (bf16[1,128,512]{2,1,0:T(8,128)(2,1)}, f32[128,512]{1,0:T(8,128)}, bf16[1,256,512]{2,1,0:T(8,128)(2,1)}, bf16[1,256,512]{2,1,0:T(8,128)(2,1)}) custom-call(bf16[1,128,512]{2,1,0:T(8,128)(2,1)S(1)} %get-tuple-element.8.refs_0_, f32[128,512]{1,0:T(8,128)S(1)} %get-tuple-element.9.refs_1_, bf16[1,256,512]{2,1,0:T(8,128)(2,1)S(1)} %get-tuple-element.10.refs_2_, ...), custom_call_target="tpu_custom_call" | custom-call | tf_op jit(solution)/shard_map/pallas_call | solution.py:414
